TPU v7x, 32 devices: a whole 2x2x4 slice. The times are simulated.
32 devices in a mesh: ens: 8 (over z, core), pen: 4 (over y, x).
Axes of the slice: x: 2, y: 2, z: 4, core: 2. Of those that a mesh axis runs over, the one named last changes fastest.
Arguments:
- state: float32 [2, 8, 4, 256, 512], P(None, 'ens', None, 'pen'), may hold values from -8 to 8, as said below
- accum: float32 [2, 8, 4, 256, 512], P(None, 'ens', None, 'pen'), may hold values from -8 to 8, as said below
- base_flow: float32 [6, 4, 256, 256], P(None, None, 'pen', 'ens'), may hold values from -6 to 6
Outputs:
- state_next: float32 [2, 8, 4, 256, 512], P(None, 'ens', None, 'pen')
- accum_next: float32 [2, 8, 4, 256, 512], P(None, 'ens', None, 'pen')
Inputs may be any that keep to these rules, and one draw needn't show every extreme that they name: `state`: each field of each perturbation and level is the spectrum of a real field: the entry at ((256 - ky) mod 256, (256 - kx) mod 256) is the complex conjugate of the entry at (ky, kx). `accum`: each field of each perturbation and level is the spectrum of a real field: the entry at ((256 - ky) mod 256, (256 - kx) mod 256) is the complex conjugate of the entry at (ky, kx).
All inputs are finite; a program needn't handle non-finite values.
Results may differ from a plain program's by a relative error of at most 0.0003.
Values sent between devices are 32-bit elements; how exact they have to be, the bound alone decides.
No kernel may reach another device: no remote copies, remote signals or barrier semaphores. Data moves between devices by JAX's collectives and lax.ppermute only.
A program may use at most 64 MiB of HBM per device.

v0:
```python
import functools
import math

import jax
import jax.numpy as jnp
import ml_dtypes
import numpy as np
from jax import lax
from jax.experimental import pallas as pl
from jax.experimental.pallas import tpu as pltpu
from jax.sharding import PartitionSpec as P

viscosity = 0.05
diffusivity = 0.05
vertical_mixing = 0.5
buoyancy_gain = 0.5
stratification = 0.5
memory_factor = -5.0 / 9.0
weight_factor = 15.0 / 16.0
time_step = 0.4


def wave_numbers(amount, offset, length):
    position = offset + jnp.arange(amount, dtype=jnp.int32)
    half_length = length // 2
    signed = jnp.where(position <= half_length, position, position - length)
    derivative = jnp.where(position == half_length, 0, signed)
    return (2.0 * math.pi / length * derivative.astype(jnp.float32), signed)


def times_i(real_part, imag_part, factor):
    return (-factor * imag_part, factor * real_part)


def vertical(quantity, level_axis):
    depth = quantity.shape[level_axis]
    lower = lax.slice_in_dim(quantity, 0, 1, axis=level_axis)
    upper = lax.slice_in_dim(quantity, depth - 1, depth, axis=level_axis)
    padded = jnp.concatenate([lower, quantity, upper], axis=level_axis)
    above = lax.slice_in_dim(padded, 2, depth + 2, axis=level_axis)
    below = lax.slice_in_dim(padded, 0, depth, axis=level_axis)
    return above + below - 2.0 * quantity


def tendency(vort, buoy, advect, across, kappa_x, square, level_axis):
    tend_vort_re = (
        -advect[0]
        + buoyancy_gain * (-kappa_x * buoy[1])
        - viscosity * square * vort[0]
        + vertical_mixing * vertical(vort[0], level_axis)
    )
    tend_vort_im = (
        -advect[1]
        + buoyancy_gain * (kappa_x * buoy[0])
        - viscosity * square * vort[1]
        + vertical_mixing * vertical(vort[1], level_axis)
    )
    tend_buoy_re = (
        -advect[2]
        - stratification * across[0]
        - diffusivity * square * buoy[0]
        + vertical_mixing * vertical(buoy[0], level_axis)
    )
    tend_buoy_im = (
        -advect[3]
        - stratification * across[1]
        - diffusivity * square * buoy[1]
        + vertical_mixing * vertical(buoy[1], level_axis)
    )
    return jnp.stack(
        [
            jnp.concatenate([tend_vort_re, tend_vort_im], axis=-1),
            jnp.concatenate([tend_buoy_re, tend_buoy_im], axis=-1),
        ]
    )


def dft_tables(length):
    position = jnp.arange(length, dtype=jnp.int32)
    product = position[:, None] * position[None, :] % length
    angle = 2.0 * math.pi / length * product.astype(jnp.float32)
    scale = 1.0 / math.sqrt(length)
    return (scale * jnp.cos(angle), scale * jnp.sin(angle))


def to_physical(spectral, x_table, y_table):
    mixed_space = jnp.einsum(
        "fplkj,jcx->fplcxk", spectral, x_table, precision=lax.Precision.HIGHEST
    )
    return jnp.einsum(
        "fplcxk,ckm->fplxm",
        lax.all_to_all(mixed_space, "pen", split_axis=4, concat_axis=5, tiled=True),
        y_table,
        precision=lax.Precision.HIGHEST,
    )


def on_device_general(state, accum, base_flow):
    grid_size = state.shape[-1] // 2
    row_count = state.shape[3]
    base_all = lax.all_gather(base_flow, "ens", axis=3, tiled=True)
    kappa_rows, signed_y = wave_numbers(row_count, lax.axis_index("pen") * row_count, grid_size)
    kappa_cols, signed_x = wave_numbers(grid_size, 0, grid_size)
    kappa_y = kappa_rows[:, None]
    kappa_x = kappa_cols[None, :]
    wave_square = signed_y[:, None] ** 2 + signed_x[None, :] ** 2
    factor = (2.0 * math.pi / grid_size) ** 2
    square = factor * wave_square.astype(jnp.float32)
    inverse = jnp.where(
        wave_square > 0, 1.0 / (factor * jnp.maximum(wave_square, 1).astype(jnp.float32)), 0.0
    )
    vort = (state[0][..., :grid_size], state[0][..., grid_size:])
    buoy = (state[1][..., :grid_size], state[1][..., grid_size:])
    potential_re = -vort[0] * inverse
    potential_im = -vort[1] * inverse
    flow_x = times_i(potential_re, potential_im, -kappa_y)
    flow_y = times_i(potential_re, potential_im, kappa_x)
    vort_x = times_i(vort[0], vort[1], kappa_x)
    vort_y = times_i(vort[0], vort[1], kappa_y)
    buoy_x = times_i(buoy[0], buoy[1], kappa_x)
    buoy_y = times_i(buoy[0], buoy[1], kappa_y)
    cosine_table, sine_table = dft_tables(grid_size)
    x_table = jnp.concatenate(
        [
            jnp.stack([cosine_table, sine_table], axis=1),
            jnp.stack([-sine_table, cosine_table], axis=1),
        ],
        axis=0,
    )
    y_table = jnp.stack([cosine_table, -sine_table])
    components = [flow_x, flow_y, vort_x, vort_y, buoy_x, buoy_y]
    spectral = jnp.stack([jnp.concatenate(component, axis=-1) for component in components])
    physical = to_physical(spectral, x_table, y_table)
    flow_x_p, flow_y_p = (physical[0], physical[1])
    vort_x_p, vort_y_p = (physical[2], physical[3])
    buoy_x_p, buoy_y_p = (physical[4], physical[5])
    advect_vort = (
        base_all[0] * vort_x_p
        + base_all[1] * vort_y_p
        + flow_x_p * base_all[2]
        + flow_y_p * base_all[3]
    )
    advect_buoy = (
        base_all[0] * buoy_x_p
        + base_all[1] * buoy_y_p
        + flow_x_p * base_all[4]
        + flow_y_p * base_all[5]
    )
    advect_both = jnp.stack([advect_vort, advect_buoy])
    y_forward = jnp.stack([cosine_table, -sine_table], axis=1)
    x_forward = jnp.stack(
        [
            jnp.concatenate([cosine_table, -sine_table], axis=1),
            jnp.concatenate([sine_table, cosine_table], axis=1),
        ]
    )
    spread = jnp.einsum(
        "fplxy,yck->fplckx", advect_both, y_forward, precision=lax.Precision.HIGHEST
    )
    spectra = jnp.einsum(
        "fplckx,cxm->fplkm",
        lax.all_to_all(spread, "pen", split_axis=4, concat_axis=5, tiled=True),
        x_forward,
        precision=lax.Precision.HIGHEST,
    )
    advect = (
        spectra[0][..., :grid_size],
        spectra[0][..., grid_size:],
        spectra[1][..., :grid_size],
        spectra[1][..., grid_size:],
    )
    tend = tendency(vort, buoy, advect, flow_y, kappa_x, square, 1)
    accum_next = memory_factor * accum + tend
    state_next = state + weight_factor * time_step * accum_next
    return (state_next, accum_next)


PEN = 4
HALF_ROWS = 32
EXTRA = 8


def split(values):
    high = values.astype(jnp.bfloat16)
    return high, (values - high.astype(jnp.float32)).astype(jnp.bfloat16)


def split_table(values):
    high = values.astype(ml_dtypes.bfloat16)
    low = (values - high.astype(np.float64)).astype(ml_dtypes.bfloat16)
    return np.stack([high, low], axis=-3)


def cosine(grid, left, right):
    return np.cos(2.0 * np.pi / grid * (left * right % grid)) / math.sqrt(grid)


def sine(grid, left, right):
    return np.sin(2.0 * np.pi / grid * (left * right % grid)) / math.sqrt(grid)


def x_forward_table(grid):
    kx = np.arange(grid)
    x = kx[:, None]
    return split_table(np.concatenate([cosine(grid, x, kx), sine(grid, x, kx)], axis=1))


def x_inverse_table(grid):
    rows = grid // PEN
    kx = np.arange(grid)[:, None]
    tables = []
    for device in range(PEN):
        x = np.concatenate([block * rows + np.arange(rows) for block in (device, device ^ 2)])
        tables.append(np.concatenate([cosine(grid, kx, x), sine(grid, kx, x)], axis=1))
    return split_table(np.stack(tables))


def row_numbers(device, rows):
    own = device * rows + np.arange(rows)
    near = [(device ^ step) * rows + np.arange(HALF_ROWS) for step in (1, 2)]
    return np.concatenate([own] + near)


def y_inverse_table(grid):
    rows = grid // PEN
    y = np.arange(grid)[:, None]
    tables = []
    for device in range(PEN):
        ky = row_numbers(device, rows)
        real = np.where(ky % (grid // 2) == 0, 1.0, 2.0) * cosine(grid, y, ky)
        imag = -2.0 * sine(grid, y, ky)
        extra = (device ^ 2) * rows + HALF_ROWS
        far = (device ^ 3) * rows
        from_y = rows + HALF_ROWS
        extra_real, extra_imag = 2.0 * cosine(grid, y[:, 0], extra), -2.0 * sine(grid, y[:, 0], extra)
        imag[:, from_y] = extra_imag
        if device % 2 == 0:
            imag[:, 0] = extra_real
        else:
            real[:, from_y] = extra_real
            imag[:, rows] = cosine(grid, y[:, 0], far)
        tables.append(np.concatenate([real, imag], axis=1))
    return split_table(np.stack(tables))


def y_forward_table(grid):
    rows = grid // PEN
    parts = []
    for device in range(PEN):
        ky = device * rows + np.arange(rows)[:, None]
        y = np.arange(grid)[None, :]
        parts += [cosine(grid, ky, y), -sine(grid, ky, y)]
    return split_table(np.concatenate(parts, axis=0))


def dot(left, right):
    return jnp.dot(left, right, preferred_element_type=jnp.float32)


def dot_split(left, right):
    return dot(left[0], right[0]) + (dot(left[1], right[0]) + dot(left[0], right[1]))


def waves(position, grid):
    signed = jnp.where(position <= grid // 2, position, position - grid)
    derivative = jnp.where(position == grid // 2, 0, signed)
    return (2.0 * math.pi / grid) * derivative.astype(jnp.float32), signed


def wave_arrays(row_position, grid):
    kappa_y, signed_y = waves(row_position, grid)
    kappa_x, signed_x = waves(lax.broadcasted_iota(jnp.int32, (1, grid), 1), grid)
    wave_square = signed_y * signed_y + signed_x * signed_x
    factor = (2.0 * math.pi / grid) ** 2
    square = factor * wave_square.astype(jnp.float32)
    inverse = jnp.where(wave_square > 0, 1.0 / jnp.where(wave_square > 0, square, 1.0), 0.0)
    return kappa_y, kappa_x, square, inverse


def interleave(even, odd):
    low_lanes = lax.broadcasted_iota(jnp.int32, (1, 128), 1) < 64
    return (
        jnp.where(low_lanes, even, pltpu.roll(odd, 64, 1)),
        jnp.where(low_lanes, pltpu.roll(even, 64, 1), odd),
    )


def base_kernel(base_ref, own_ref, swap_ref):
    mine = (lax.axis_index("pen") // 2) * 2
    for out_ref, first in ((own_ref, mine), (swap_ref, 2 - mine)):
        for field in range(base_ref.shape[0]):
            out_ref[:, 128 * field : 128 * field + 128] = jnp.concatenate(
                [base_ref[field, first], base_ref[field, first + 1]], axis=1
            )


def state_kernel(state_ref, near_x_ref, near_y_ref, far_ref):
    mine = (lax.axis_index("pen") // 2) * 2
    far_ref[...] = jnp.zeros_like(far_ref)
    near_y_ref[4 * HALF_ROWS :, :] = jnp.zeros((EXTRA, near_y_ref.shape[1]), jnp.float32)
    for field in range(2):
        for level in range(2):
            index = 2 * field + level
            place = slice(HALF_ROWS * index, HALF_ROWS * (index + 1))
            near_x_ref[place, :] = state_ref[field, 0, mine + level, :HALF_ROWS, :]
            other = 2 - mine + level
            near_y_ref[place, :] = state_ref[field, 0, other, :HALF_ROWS, :]
            line = slice(4 * HALF_ROWS + index, 4 * HALF_ROWS + index + 1)
            near_y_ref[line, :] = state_ref[field, 0, other, HALF_ROWS : HALF_ROWS + 1, :]
            far_ref[index : index + 1, :] = state_ref[field, 0, other, 0:1, :]


def inverse_kernel(
    grid, state_ref, near_x_ref, near_y_ref, far_ref, x_ref, y_ref, own_ref, swap_ref, held, mixed, high_ref, low_ref
):
    rows = state_ref.shape[3]
    pen = lax.axis_index("pen")
    mine = (pen // 2) * 2
    odd = pen % 2 == 1
    count = 2 * rows + EXTRA
    for field in range(2):
        for level in range(2):
            index = 2 * field + level
            place = slice(HALF_ROWS * index, HALF_ROWS * (index + 1))
            held[index, :rows, :] = state_ref[field, 0, mine + level]
            held[index, rows : rows + HALF_ROWS, :] = near_x_ref[place, :]
            held[index, rows + HALF_ROWS : 2 * rows, :] = near_y_ref[place, :]
            held[index, 2 * rows :, :] = jnp.zeros((EXTRA, 2 * grid), jnp.float32)
            line = slice(4 * HALF_ROWS + index, 4 * HALF_ROWS + index + 1)
            held[index, 2 * rows : 2 * rows + 1, :] = near_y_ref[line, :]
            held[index, 2 * rows + 1 : 2 * rows + 2, :] = far_ref[index : index + 1, :]
    row = lax.broadcasted_iota(jnp.int32, (count, 1), 0)
    ky = jnp.where(
        row < rows,
        pen * rows + row,
        jnp.where(
            row < rows + HALF_ROWS,
            (pen ^ 1) * rows + row - rows,
            jnp.where(
                row <= 2 * rows, (pen ^ 2) * rows + row - rows - HALF_ROWS, (pen ^ 3) * rows
            ),
        ),
    )
    kappa_y, kappa_x, _, inverse = wave_arrays(ky, grid)
    table = (x_ref[pen, 0], x_ref[pen, 1])
    fields = [
        (0, inverse, kappa_y),
        (0, -kappa_x * inverse, None),
        (0, kappa_x, None),
        (0, None, kappa_y),
        (1, kappa_x, None),
        (1, None, kappa_y),
    ]
    for number, (field, before, after) in enumerate(fields):
        stacked = []
        for level in range(2):
            for columns in (slice(0, grid), slice(grid, 2 * grid)):
                values = held[2 * field + level, :, columns]
                stacked.append(values if before is None else values * before)
        product = dot_split(split(jnp.concatenate(stacked, axis=0)), table)
        for level in range(2):
            top = product[2 * level * count : (2 * level + 1) * count]
            bottom = product[(2 * level + 1) * count : (2 * level + 2) * count]
            real = -(bottom[:, :128] + top[:, 128:])
            imag = top[:, :128] - bottom[:, 128:]
            if after is not None:
                real, imag = after * real, after * imag
            mixed[level, : 2 * rows, :] = real[: 2 * rows]
            mixed[level, 2 * rows :, :] = imag[: 2 * rows]
            extra_real, extra_imag = real[2 * rows : 2 * rows + 1], imag[2 * rows : 2 * rows + 1]
            far_real = real[2 * rows + 1 : 2 * rows + 2]
            from_y = rows + HALF_ROWS
            mixed[level, from_y : from_y + 1, :] = jnp.where(
                odd, extra_real, real[from_y : from_y + 1]
            )
            mixed[level, 2 * rows : 2 * rows + 1, :] = jnp.where(odd, imag[0:1], extra_real)
            mixed[level, 3 * rows : 3 * rows + 1, :] = jnp.where(
                odd, far_real, imag[rows : rows + 1]
            )
            mixed[level, 2 * rows + from_y : 2 * rows + from_y + 1, :] = extra_imag
        for block, values in enumerate(interleave(mixed[0], mixed[1])):
            high, low = split(values)
            high_ref[block, :, 128 * number : 128 * number + 128] = high
            low_ref[block, :, 128 * number : 128 * number + 128] = low
    left = (y_ref[pen, 0], y_ref[pen, 1])
    own_ref[...] = dot_split(left, (high_ref[0], low_ref[0]))
    swap_ref[...] = dot_split(left, (high_ref[1], low_ref[1]))


def advection_kernel(masks, rows, field_ref, *refs):
    blocks, forward_ref = refs[: len(masks)], refs[len(masks)]
    outs, (high_ref, low_ref) = refs[len(masks) + 1 : len(masks) + 1 + PEN], refs[-2:]
    ens = lax.axis_index("ens")
    for (mask, slot), block in zip(masks, blocks, strict=True):
        tall = block.shape[-2]
        place = pl.ds(pl.multiple_of((ens ^ mask) * tall, tall), tall)

        def base(index, block=block, slot=slot):
            lanes = slice(128 * index, 128 * index + 128)
            return block[:, lanes] if slot is None else block[slot, :, lanes]

        def field(index, place=place):
            return field_ref[place, 128 * index : 128 * index + 128]

        for output, first in ((0, 2), (1, 4)):
            total = (
                base(0) * field(first)
                + base(1) * field(first + 1)
                + field(0) * base(first)
                + field(1) * base(first + 1)
            )
            high, low = split(total)
            high_ref[place, 128 * output : 128 * output + 128] = high
            low_ref[place, 128 * output : 128 * output + 128] = low
    pen = lax.axis_index("pen")
    for step in range(PEN):
        place = pl.ds(pl.multiple_of((pen ^ step) * 2 * rows, 2 * rows), 2 * rows)
        outs[step][...] = dot_split(
            (forward_ref[0, place, :], forward_ref[1, place, :]), (high_ref[...], low_ref[...])
        )


def x_forward(chunk, messages, gathered, table_ref, rows):
    pen = lax.axis_index("pen")
    for step in range(PEN):
        gathered[pen ^ step] = messages[step][...]
    grid = table_ref.shape[1]
    for pair in range(2):
        block = pair if chunk == 0 else 1 - pair
        lines = slice(2 * rows * block, 2 * rows * (block + 1))
        stacked = []
        for field in range(2):
            lanes = slice(128 * field, 128 * field + 128)
            stacked += interleave(gathered[2 * pair, :, lanes], gathered[2 * pair + 1, :, lanes])
        product = dot_split(
            split(jnp.concatenate(stacked, axis=0)), (table_ref[0, lines, :], table_ref[1, lines, :])
        )
        for index in range(4):
            top = product[2 * index * rows : (2 * index + 1) * rows]
            bottom = product[(2 * index + 1) * rows : (2 * index + 2) * rows]
            yield (
                index // 2,
                2 * pair + index % 2,
                top[:, :grid] + bottom[:, grid:],
                bottom[:, :grid] - top[:, grid:],
            )


def first_kernel(grid, *refs):
    messages, (state_ref, accum_ref, table_ref, out_ref, gathered) = refs[:PEN], refs[PEN:]
    rows, levels = state_ref.shape[3], state_ref.shape[2]
    row = lax.broadcasted_iota(jnp.int32, (rows, 1), 0)
    _, kappa_x, square, inverse = wave_arrays(lax.axis_index("pen") * rows + row, grid)
    real, imag = slice(0, grid), slice(grid, 2 * grid)
    for field, level, advect_real, advect_imag in x_forward(0, messages, gathered, table_ref, rows):
        for columns, other, sign, advect in (
            (real, imag, 1.0, advect_real),
            (imag, real, -1.0, advect_imag),
        ):
            here = state_ref[field, 0, level, :, columns]
            above = state_ref[field, 0, min(level + 1, levels - 1), :, columns]
            below = state_ref[field, 0, max(level - 1, 0), :, columns]
            cross = state_ref[1 - field, 0, level, :, other]
            if field == 0:
                coupling = (-sign * buoyancy_gain) * (kappa_x * cross)
            else:
                coupling = (-sign * stratification) * (kappa_x * inverse * cross)
            damping = viscosity if field == 0 else diffusivity
            out_ref[field, 0, level, :, columns] = (
                memory_factor * accum_ref[field, 0, level, :, columns]
                - advect
                + coupling
                - damping * square * here
                + vertical_mixing * (above + below - 2.0 * here)
            )


def second_kernel(grid, *refs):
    messages, (state_ref, part_ref, table_ref, state_out, accum_out, gathered) = refs[:PEN], refs[PEN:]
    rows = state_ref.shape[3]
    for field, level, *advect in x_forward(1, messages, gathered, table_ref, rows):
        for columns, values in zip((slice(0, grid), slice(grid, 2 * grid)), advect, strict=True):
            memory = part_ref[field, 0, level, :, columns] - values
            accum_out[field, 0, level, :, columns] = memory
            state_out[field, 0, level, :, columns] = (
                state_ref[field, 0, level, :, columns] + weight_factor * time_step * memory
            )


def pack_kernel(*refs):
    for index, ref in enumerate(refs[:-1]):
        refs[-1][index] = ref[...]


def call(kernel, outs, scratch, flops, args, limit=40):
    total = sum(math.prod(a.shape) * a.dtype.itemsize for a in list(args) + list(outs))
    return pl.pallas_call(
        kernel,
        out_shape=outs,
        in_specs=[pl.BlockSpec(memory_space=pltpu.VMEM)] * len(args),
        out_specs=[pl.BlockSpec(memory_space=pltpu.VMEM)] * len(outs),
        scratch_shapes=scratch,
        compiler_params=pltpu.CompilerParams(vmem_limit_bytes=limit * 1024 * 1024),
        cost_estimate=pl.CostEstimate(flops=flops, bytes_accessed=total, transcendentals=0),
    )(*args)


def exchange(values, axis, size, mask):
    return lax.ppermute(values, axis, [(index, index ^ mask) for index in range(size)])


def gather_blocks(block, size):
    held = {0: block}
    bit = size // 2
    while bit > 1:
        for offset in list(held):
            mask = 2 * bit - 2
            held[offset ^ mask] = exchange(held[offset], "ens", size, mask)
        bit //= 2
    offsets = list(held)
    early, last = offsets[:-1], offsets[-1]
    shape = jax.ShapeDtypeStruct((len(early),) + block.shape, block.dtype)
    (packed,) = call(pack_kernel, [shape], [], 0, [held[offset] for offset in early])
    packed = exchange(packed, "ens", size, 1)
    final = exchange(held[last], "ens", size, 1)
    found = [((offset, None), held[offset]) for offset in offsets]
    found += [((offset ^ 1, slot), packed) for slot, offset in enumerate(early)]
    found.append(((last ^ 1, None), final))
    return found


def on_device(axes, state, accum, base_flow):
    grid, rows, levels = state.shape[-1] // 2, state.shape[3], state.shape[2]
    size = axes["ens"]
    if axes["pen"] != PEN or levels != 4 or grid != 256 or size & (size - 1):
        return on_device_general(state, accum, base_flow)
    f32, bf16 = jnp.float32, jnp.bfloat16
    shape = functools.partial(jax.ShapeDtypeStruct, dtype=f32)
    fields, _, wide, tall = base_flow.shape
    lanes = 2 * wide
    x_forward_parts = jnp.asarray(x_forward_table(grid))

    own_base, swap_base = call(
        base_kernel,
        [shape((tall, fields * lanes))] * 2,
        [],
        0,
        [jnp.swapaxes(base_flow, 2, 3)],
    )
    own_blocks = gather_blocks(own_base, size)
    swap_blocks = gather_blocks(exchange(swap_base, "pen", PEN, 2), size)
    near_x, near_y, far = call(
        state_kernel,
        [
            shape((4 * HALF_ROWS, 2 * grid)),
            shape((4 * HALF_ROWS + EXTRA, 2 * grid)),
            shape((EXTRA, 2 * grid)),
        ],
        [],
        0,
        [state],
    )
    near_x = exchange(near_x, "pen", PEN, 1)
    near_y = exchange(near_y, "pen", PEN, 2)
    far = exchange(far, "pen", PEN, 3)
    count = 2 * rows + EXTRA
    own_fields, swap_fields = call(
        functools.partial(inverse_kernel, grid),
        [shape((grid, fields * lanes))] * 2,
        [
            pltpu.VMEM((4, count, 2 * grid), f32),
            pltpu.VMEM((2, 4 * rows, lanes), f32),
            pltpu.VMEM((2, grid, fields * lanes), bf16),
            pltpu.VMEM((2, grid, fields * lanes), bf16),
        ],
        6 * fields * 4 * count * grid * 256 + 12 * grid * grid * fields * lanes,
        [
            state,
            near_x,
            near_y,
            far,
            jnp.asarray(x_inverse_table(grid)),
            jnp.asarray(y_inverse_table(grid)),
        ],
    )
    back = []
    forward = jnp.asarray(y_forward_table(grid))
    for physical, blocks in ((own_fields, own_blocks), (swap_fields, swap_blocks)):
        masks = tuple(key for key, _ in blocks)
        parts = call(
            functools.partial(advection_kernel, masks, rows),
            [shape((2 * rows, 2 * lanes))] * PEN,
            [pltpu.VMEM((grid, 2 * lanes), bf16)] * 2,
            6 * 2 * grid * grid * 2 * lanes,
            [physical] + [block for _, block in blocks] + [forward],
        )
        back.append([parts[0]] + [exchange(parts[step], "pen", PEN, step) for step in range(1, PEN)])
    gathered = [pltpu.VMEM((PEN, 2 * rows, 2 * lanes), f32)]
    flops = 6 * 8 * 2 * rows * 2 * rows * 2 * grid
    (part,) = call(
        functools.partial(first_kernel, grid),
        [shape(state.shape)],
        gathered,
        flops,
        back[0] + [state, accum, x_forward_parts],
    )
    state_next, accum_next = call(
        functools.partial(second_kernel, grid),
        [shape(state.shape), shape(state.shape)],
        gathered,
        flops,
        back[1] + [state, part, x_forward_parts],
    )
    return state_next, accum_next


def solution(mesh):
    return jax.shard_map(
        functools.partial(on_device, dict(mesh.shape)),
        mesh=mesh,
        in_specs=(
            P(None, "ens", None, "pen", None),
            P(None, "ens", None, "pen", None),
            P(None, None, "pen", "ens"),
        ),
        out_specs=(P(None, "ens", None, "pen", None), P(None, "ens", None, "pen", None)),
        check_vma=False,
    )
```

profile of v0, /device:TPU:0, one launch (start us, length us, event | category | flops | bytes accessed | tf_op | source)
XLA Modules:
  0.0 50.9 jit_solution(13346700511985536900)
XLA Ops:
  0.6 0.0 copy-start.5
  0.6 1.0 %copy-done.5 = f32[6,4,64,32]{2,3,1,0:T(8,128)S(1)} copy-done((f32[6,4,64,32]{2,3,1,0:T(8,128)S(1)}, f32[6,4,64,32]{2,3,1,0:T(8,128)}, u32[]{:S(2)}) %copy-start.5) | copy-done | bytes 196632
  1.6 0.1 shard_map.88
  1.7 3.0 %collective-permute-start.3 = (f32[32,768]{1,0:T(8,128)S(1)}, f32[32,768]{1,0:T(8,128)S(1)}, u32[]{:S(2)}, u32[]{:S(2)}) collective-permute-start(f32[32,768]{1,0:T(8,128)S(1)} %get-tuple-element.21), channel_id=1, source_target_pairs={{0,2},{1,3},{2,0},{3,1},{4,6},{5,7},{6,4},{7,5},{8,10},{9,11},{10,... | collective-permute-start | bytes 294920 | tf_op jit(solution)/shard_map/ppermute | solution.py:509
  4.8 0.0 copy-start
  4.8 1.2 %copy-done = f32[2,1,4,64,512]{4,3,2,1,0:T(8,128)S(1)} copy-done((f32[2,1,4,64,512]{4,3,2,1,0:T(8,128)S(1)}, f32[2,1,4,64,512]{4,3,2,1,0:T(8,128)}, u32[]{:S(2)}) %copy-start) | copy-done | bytes 1048600
  6.0 0.0 copy-start.1
  6.0 0.0 copy-start.6
  6.1 0.1 collective-permute-start.1
  6.1 2.0 %collective-permute-start = (f32[128,512]{1,0:T(8,128)S(1)}, f32[128,512]{1,0:T(8,128)S(1)}, u32[]{:S(2)}, u32[]{:S(2)}) collective-permute-start(f32[128,512]{1,0:T(8,128)S(1)} %get-tuple-element.17), channel_id=1, source_target_pairs={{0,1},{1,0},{2,3},{3,2},{4,5},{5,4},{6,7},{7,6},{8,9},{9,8},{10,11... | collective-permute-start | bytes 786440 | tf_op jit(solution)/shard_map/ppermute | solution.py:509
  8.1 3.6 %collective-permute-start.12 = (f32[32,768]{1,0:T(8,128)S(1)}, f32[32,768]{1,0:T(8,128)S(1)}, u32[]{:S(2)}, u32[]{:S(2)}) collective-permute-start(f32[32,768]{1,0:T(8,128)S(1)} %get-tuple-element.27.refs_0_), channel_id=1, source_target_pairs={{0,24},{4,28},{8,16},{12,20},{16,8},{20,12},{24,0},{28,4},{1,25},{... | collective-permute-start | bytes 294920 | tf_op jit(solution)/shard_map/ppermute | solution.py:509
  11.7 0.0 collective-permute-start.13
  11.7 0.0 collective-permute-done.3.refs_0_
  11.7 0.9 %collective-permute-start.4 = (f32[32,768]{1,0:T(8,128)S(1)}, f32[32,768]{1,0:T(8,128)S(1)}, u32[]{:S(2)}, u32[]{:S(2)}) collective-permute-start(f32[32,768]{1,0:T(8,128)S(1)} %collective-permute-done.3.refs_0_), channel_id=1, source_target_pairs={{0,24},{4,28},{8,16},{12,20},{16,8},{20,12},{24,0},{28,4},{1,25},{... | collective-permute-start | bytes 294920 | tf_op jit(solution)/shard_map/ppermute | solution.py:509
  12.6 2.4 %collective-permute-done.12.refs_1_ = f32[32,768]{1,0:T(8,128)S(1)} collective-permute-done((f32[32,768]{1,0:T(8,128)S(1)}, f32[32,768]{1,0:T(8,128)S(1)}, u32[]{:S(2)}, u32[]{:S(2)}) %collective-permute-start.12) | collective-permute-done | bytes 98336 | tf_op jit(solution)/shard_map/ppermute | solution.py:509
  15.0 3.3 %collective-permute-done.13.refs_2_ = f32[32,768]{1,0:T(8,128)S(1)} collective-permute-done((f32[32,768]{1,0:T(8,128)S(1)}, f32[32,768]{1,0:T(8,128)S(1)}, u32[]{:S(2)}, u32[]{:S(2)}) %collective-permute-start.13) | collective-permute-done | bytes 98336 | tf_op jit(solution)/shard_map/ppermute | solution.py:509
  18.3 0.1 collective-permute-start.15
  18.4 0.4 collective-permute-start.5
  18.8 0.0 collective-permute-done.4.refs_1_
  18.8 1.7 %collective-permute-start.14 = (f32[32,768]{1,0:T(8,128)S(1)}, f32[32,768]{1,0:T(8,128)S(1)}, u32[]{:S(2)}, u32[]{:S(2)}) collective-permute-start(f32[32,768]{1,0:T(8,128)S(1)} %collective-permute-done.12.refs_1_), channel_id=1, source_target_pairs={{0,8},{4,12},{8,0},{12,4},{16,24},{20,28},{24,16},{28,20},{1,9},{5... | collective-permute-start | bytes 294920 | tf_op jit(solution)/shard_map/ppermute | solution.py:509
  20.5 3.6 %collective-permute-done.5.refs_2_ = f32[32,768]{1,0:T(8,128)S(1)} collective-permute-done((f32[32,768]{1,0:T(8,128)S(1)}, f32[32,768]{1,0:T(8,128)S(1)}, u32[]{:S(2)}, u32[]{:S(2)}) %collective-permute-start.5) | collective-permute-done | bytes 98336 | tf_op jit(solution)/shard_map/ppermute | solution.py:509
  24.1 1.5 %collective-permute-start.2 = (f32[8,512]{1,0:T(8,128)S(1)}, f32[8,512]{1,0:T(8,128)S(1)}, u32[]{:S(2)}, u32[]{:S(2)}) collective-permute-start(f32[8,512]{1,0:T(8,128)S(1)} %get-tuple-element.19), channel_id=1, source_target_pairs={{0,3},{1,2},{2,1},{3,0},{4,7},{5,6},{6,5},{7,4},{8,11},{9,10},{10,... | collective-permute-start | bytes 49160 | tf_op jit(solution)/shard_map/ppermute | solution.py:509
  25.6 0.0 copy-start.2
  25.6 3.1 %collective-permute-done.2.far_ref = f32[8,512]{1,0:T(8,128)S(1)} collective-permute-done((f32[8,512]{1,0:T(8,128)S(1)}, f32[8,512]{1,0:T(8,128)S(1)}, u32[]{:S(2)}, u32[]{:S(2)}) %collective-permute-start.2) | collective-permute-done | bytes 16416 | tf_op jit(solution)/shard_map/ppermute | solution.py:509
  28.7 0.0 collective-permute-start.7
  28.7 0.0 collective-permute-done.14.refs_3_
  28.7 0.3 collective-permute-start.6
  29.0 0.0 collective-permute-done.near_x_ref
  29.0 0.3 collective-permute-start.16
  29.3 0.0 collective-permute-done.1.near_y_ref
  29.3 0.0 copy-done.1
  29.3 0.0 copy-done.6
  29.3 0.0 copy-start.7
  29.3 1.2 %copy-done.7 = bf16[4,2,256,256]{3,2,1,0:T(8,128)(2,1)S(1)} copy-done((bf16[4,2,256,256]{3,2,1,0:T(8,128)(2,1)S(1)}, bf16[4,2,256,256]{3,2,1,0:T(8,128)(2,1)}, u32[]{:S(2)}) %copy-start.7) | copy-done | bytes 1048600
  30.5 2.5 %shard_map.87 = (f32[256,768]{1,0:T(8,128)S(1)}, f32[256,768]{1,0:T(8,128)S(1)}) custom-call(f32[2,1,4,64,512]{4,3,2,1,0:T(8,128)S(1)} %copy-done.1, f32[128,512]{1,0:T(8,128)S(1)} %collective-permute-done.near_x_ref, f32[136,512]{1,0:T(8,128)S(1)} %collective-permute-done.1.near_y_ref, f32[8,512]{1,0:T(8,128)S(1)} %collective-permute-done.2.far_ref, ...), custom_call_target="tpu_custom_call" | custom-call | flops 1887436800 | bytes 5275648 | tf_op jit(solution)/shard_map/pallas_call | solution.py:497
  33.0 0.0 collective-permute-done.16.refs_7_
  33.0 0.0 collective-permute-done.15.refs_4_.refs_5_.refs_6_
  33.0 0.0 copy-done.2
  33.1 0.5 shard_map.92
  33.6 0.6 %collective-permute-start.17 = (f32[128,256]{1,0:T(8,128)S(1)}, f32[128,256]{1,0:T(8,128)S(1)}, u32[]{:S(2)}, u32[]{:S(2)}) collective-permute-start(f32[128,256]{1,0:T(8,128)S(1)} %get-tuple-element.29), channel_id=1, source_target_pairs={{0,1},{1,0},{2,3},{3,2},{4,5},{5,4},{6,7},{7,6},{8,9},{9,8},{10,11... | collective-permute-start | bytes 393224 | tf_op jit(solution)/shard_map/ppermute | solution.py:509
  34.1 0.0 collective-permute-done.6.refs_3_
  34.2 0.0 collective-permute-start.8
  34.2 1.5 %collective-permute-start.18 = (f32[128,256]{1,0:T(8,128)S(1)}, f32[128,256]{1,0:T(8,128)S(1)}, u32[]{:S(2)}, u32[]{:S(2)}) collective-permute-start(f32[128,256]{1,0:T(8,128)S(1)} %get-tuple-element.30), channel_id=1, source_target_pairs={{0,2},{1,3},{2,0},{3,1},{4,6},{5,7},{6,4},{7,5},{8,10},{9,11},{10,... | collective-permute-start | bytes 393224 | tf_op jit(solution)/shard_map/ppermute | solution.py:509
  35.7 1.4 %collective-permute-start.19 = (f32[128,256]{1,0:T(8,128)S(1)}, f32[128,256]{1,0:T(8,128)S(1)}, u32[]{:S(2)}, u32[]{:S(2)}) collective-permute-start(f32[128,256]{1,0:T(8,128)S(1)} %get-tuple-element.31), channel_id=1, source_target_pairs={{0,3},{1,2},{2,1},{3,0},{4,7},{5,6},{6,5},{7,4},{8,11},{9,10},{10,... | collective-permute-start | bytes 393224 | tf_op jit(solution)/shard_map/ppermute | solution.py:509
  37.1 0.0 collective-permute-done.8.refs_7_
  37.1 0.0 collective-permute-done.7.refs_4_.refs_5_.refs_6_
  37.1 0.0 copy-start.3
  37.1 0.0 copy-start.4
  37.1 0.5 shard_map.90
  37.6 1.6 %collective-permute-start.10 = (f32[128,256]{1,0:T(8,128)S(1)}, f32[128,256]{1,0:T(8,128)S(1)}, u32[]{:S(2)}, u32[]{:S(2)}) collective-permute-start(f32[128,256]{1,0:T(8,128)S(1)} %get-tuple-element.24), channel_id=1, source_target_pairs={{0,2},{1,3},{2,0},{3,1},{4,6},{5,7},{6,4},{7,5},{8,10},{9,11},{10,... | collective-permute-start | bytes 393224 | tf_op jit(solution)/shard_map/ppermute | solution.py:509
  39.2 0.5 collective-permute-start.11
  39.7 0.2 collective-permute-done.17.refs_1_
  39.9 1.3 %collective-permute-start.9 = (f32[128,256]{1,0:T(8,128)S(1)}, f32[128,256]{1,0:T(8,128)S(1)}, u32[]{:S(2)}, u32[]{:S(2)}) collective-permute-start(f32[128,256]{1,0:T(8,128)S(1)} %get-tuple-element.23), channel_id=1, source_target_pairs={{0,1},{1,0},{2,3},{3,2},{4,5},{5,4},{6,7},{7,6},{8,9},{9,8},{10,11... | collective-permute-start | bytes 393224 | tf_op jit(solution)/shard_map/ppermute | solution.py:509
  41.2 3.8 %collective-permute-done.18.refs_2_ = f32[128,256]{1,0:T(8,128)S(1)} collective-permute-done((f32[128,256]{1,0:T(8,128)S(1)}, f32[128,256]{1,0:T(8,128)S(1)}, u32[]{:S(2)}, u32[]{:S(2)}) %collective-permute-start.18) | collective-permute-done | bytes 131104 | tf_op jit(solution)/shard_map/ppermute | solution.py:509
  45.0 0.0 collective-permute-done.19.refs_3_
  45.0 0.0 copy-done.3
  45.0 0.0 copy-done.4
  45.0 1.4 %shard_map.93.refs_5_ = f32[2,1,4,64,512]{4,3,2,1,0:T(8,128)S(1)} custom-call(f32[128,256]{1,0:T(8,128)S(1)} %get-tuple-element.28.refs_0_, f32[128,256]{1,0:T(8,128)S(1)} %collective-permute-done.17.refs_1_, f32[128,256]{1,0:T(8,128)S(1)} %collective-permute-done.18.refs_2_, f32[128,256]{1,0:T(8,128)S(1)} %collective-permute-done.19.refs_3_, ...), custom_call_target="tpu_custom_call" | custom-call | flops 402653184 | bytes 4194304 | tf_op jit(solution)/shard_map/pallas_call | solution.py:497
  46.4 2.1 %collective-permute-done.10.refs_2_ = f32[128,256]{1,0:T(8,128)S(1)} collective-permute-done((f32[128,256]{1,0:T(8,128)S(1)}, f32[128,256]{1,0:T(8,128)S(1)}, u32[]{:S(2)}, u32[]{:S(2)}) %collective-permute-start.10) | collective-permute-done | bytes 131104 | tf_op jit(solution)/shard_map/ppermute | solution.py:509
  48.5 0.0 collective-permute-done.11.refs_3_
  48.5 0.0 collective-permute-done.9.refs_1_
  48.5 2.4 %shard_map.94 = (f32[2,1,4,64,512]{4,3,2,1,0:T(8,128)}, f32[2,1,4,64,512]{4,3,2,1,0:T(8,128)}) custom-call(f32[128,256]{1,0:T(8,128)S(1)} %get-tuple-element.22.refs_0_, f32[128,256]{1,0:T(8,128)S(1)} %collective-permute-done.9.refs_1_, f32[128,256]{1,0:T(8,128)S(1)} %collective-permute-done.10.refs_2_, f32[128,256]{1,0:T(8,128)S(1)} %collective-permute-done.11.refs_3_, ...), custom_call_target="tpu_custom_call" | custom-call | flops 402653184 | bytes 5242880 | tf_op jit(solution)/shard_map/pallas_call | solution.py:497
  (3 shorter events, 0.1 us)
Async XLA Ops:
  0.6 1.0 %copy-start.5 = (f32[6,4,64,32]{2,3,1,0:T(8,128)S(1)}, f32[6,4,64,32]{2,3,1,0:T(8,128)}, u32[]{:S(2)}) copy-start(f32[6,4,64,32]{2,3,1,0:T(8,128)} %param.9) | copy-start | bytes 589828
  1.7 10.0 %collective-permute-start.3 = (f32[32,768]{1,0:T(8,128)S(1)}, f32[32,768]{1,0:T(8,128)S(1)}, u32[]{:S(2)}, u32[]{:S(2)}) collective-permute-start(f32[32,768]{1,0:T(8,128)S(1)} %get-tuple-element.21), channel_id=1, source_target_pairs={{0,2},{1,3},{2,0},{3,1},{4,6},{5,7},{6,4},{7,5},{8,10},{9,11},{10,... | collective-permute-start | bytes 294920 | tf_op jit(solution)/shard_map/ppermute | solution.py:509
  4.8 1.2 %copy-start = (f32[2,1,4,64,512]{4,3,2,1,0:T(8,128)S(1)}, f32[2,1,4,64,512]{4,3,2,1,0:T(8,128)}, u32[]{:S(2)}) copy-start(f32[2,1,4,64,512]{4,3,2,1,0:T(8,128)} %refs_4_.3) | copy-start | bytes 3145732
  6.0 23.3 %copy-start.1 = (f32[2,1,4,64,512]{4,3,2,1,0:T(8,128)S(1)}, f32[2,1,4,64,512]{4,3,2,1,0:T(8,128)}, u32[]{:S(2)}) copy-start(f32[2,1,4,64,512]{4,3,2,1,0:T(8,128)} %refs_4_.3) | copy-start | bytes 3145732
  6.0 23.3 %copy-start.6 = (bf16[4,2,256,256]{3,2,1,0:T(8,128)(2,1)S(1)}, bf16[4,2,256,256]{3,2,1,0:T(8,128)(2,1)}, u32[]{:S(2)}) copy-start(bf16[4,2,256,256]{3,2,1,0:T(8,128)(2,1)} %constant.10.clone.y_ref) | copy-start | bytes 3145732
  6.1 23.2 %collective-permute-start.1 = (f32[136,512]{1,0:T(8,128)S(1)}, f32[136,512]{1,0:T(8,128)S(1)}, u32[]{:S(2)}, u32[]{:S(2)}) collective-permute-start(f32[136,512]{1,0:T(8,128)S(1)} %get-tuple-element.18), channel_id=1, source_target_pairs={{0,2},{1,3},{2,0},{3,1},{4,6},{5,7},{6,4},{7,5},{8,10},{9,11},{10,... | collective-permute-start | bytes 835592 | tf_op jit(solution)/shard_map/ppermute | solution.py:509
  6.1 22.9 %collective-permute-start = (f32[128,512]{1,0:T(8,128)S(1)}, f32[128,512]{1,0:T(8,128)S(1)}, u32[]{:S(2)}, u32[]{:S(2)}) collective-permute-start(f32[128,512]{1,0:T(8,128)S(1)} %get-tuple-element.17), channel_id=1, source_target_pairs={{0,1},{1,0},{2,3},{3,2},{4,5},{5,4},{6,7},{7,6},{8,9},{9,8},{10,11... | collective-permute-start | bytes 786440 | tf_op jit(solution)/shard_map/ppermute | solution.py:509
  8.1 6.9 %collective-permute-start.12 = (f32[32,768]{1,0:T(8,128)S(1)}, f32[32,768]{1,0:T(8,128)S(1)}, u32[]{:S(2)}, u32[]{:S(2)}) collective-permute-start(f32[32,768]{1,0:T(8,128)S(1)} %get-tuple-element.27.refs_0_), channel_id=1, source_target_pairs={{0,24},{4,28},{8,16},{12,20},{16,8},{20,12},{24,0},{28,4},{1,25},{... | collective-permute-start | bytes 294920 | tf_op jit(solution)/shard_map/ppermute | solution.py:509
  11.7 6.6 %collective-permute-start.13 = (f32[32,768]{1,0:T(8,128)S(1)}, f32[32,768]{1,0:T(8,128)S(1)}, u32[]{:S(2)}, u32[]{:S(2)}) collective-permute-start(f32[32,768]{1,0:T(8,128)S(1)} %get-tuple-element.27.refs_0_), channel_id=1, source_target_pairs={{0,8},{4,12},{8,0},{12,4},{16,24},{20,28},{24,16},{28,20},{1,9},{5... | collective-permute-start | bytes 294920 | tf_op jit(solution)/shard_map/ppermute | solution.py:509
  11.7 7.1 %collective-permute-start.4 = (f32[32,768]{1,0:T(8,128)S(1)}, f32[32,768]{1,0:T(8,128)S(1)}, u32[]{:S(2)}, u32[]{:S(2)}) collective-permute-start(f32[32,768]{1,0:T(8,128)S(1)} %collective-permute-done.3.refs_0_), channel_id=1, source_target_pairs={{0,24},{4,28},{8,16},{12,20},{16,8},{20,12},{24,0},{28,4},{1,25},{... | collective-permute-start | bytes 294920 | tf_op jit(solution)/shard_map/ppermute | solution.py:509
  18.3 14.7 %collective-permute-start.15 = (f32[3,32,768]{2,1,0:T(8,128)S(1)}, f32[3,32,768]{2,1,0:T(8,128)S(1)}, u32[]{:S(2)}, u32[]{:S(2)}) collective-permute-start(f32[3,32,768]{2,1,0:T(8,128)S(1)} %shard_map.91), channel_id=1, source_target_pairs={{0,4},{4,0},{8,12},{12,8},{16,20},{20,16},{24,28},{28,24},{1,5},{5... | collective-permute-start | bytes 884744 | tf_op jit(solution)/shard_map/ppermute | solution.py:509
  18.4 5.7 %collective-permute-start.5 = (f32[32,768]{1,0:T(8,128)S(1)}, f32[32,768]{1,0:T(8,128)S(1)}, u32[]{:S(2)}, u32[]{:S(2)}) collective-permute-start(f32[32,768]{1,0:T(8,128)S(1)} %collective-permute-done.3.refs_0_), channel_id=1, source_target_pairs={{0,8},{4,12},{8,0},{12,4},{16,24},{20,28},{24,16},{28,20},{1,9},{5... | collective-permute-start | bytes 294920 | tf_op jit(solution)/shard_map/ppermute | solution.py:509
  18.8 9.9 %collective-permute-start.14 = (f32[32,768]{1,0:T(8,128)S(1)}, f32[32,768]{1,0:T(8,128)S(1)}, u32[]{:S(2)}, u32[]{:S(2)}) collective-permute-start(f32[32,768]{1,0:T(8,128)S(1)} %collective-permute-done.12.refs_1_), channel_id=1, source_target_pairs={{0,8},{4,12},{8,0},{12,4},{16,24},{20,28},{24,16},{28,20},{1,9},{5... | collective-permute-start | bytes 294920 | tf_op jit(solution)/shard_map/ppermute | solution.py:509
  24.1 4.6 %collective-permute-start.2 = (f32[8,512]{1,0:T(8,128)S(1)}, f32[8,512]{1,0:T(8,128)S(1)}, u32[]{:S(2)}, u32[]{:S(2)}) collective-permute-start(f32[8,512]{1,0:T(8,128)S(1)} %get-tuple-element.19), channel_id=1, source_target_pairs={{0,3},{1,2},{2,1},{3,0},{4,7},{5,6},{6,5},{7,4},{8,11},{9,10},{10,... | collective-permute-start | bytes 49160 | tf_op jit(solution)/shard_map/ppermute | solution.py:509
  25.6 7.5 %copy-start.2 = (bf16[2,512,256]{2,1,0:T(8,128)(2,1)S(1)}, bf16[2,512,256]{2,1,0:T(8,128)(2,1)}, u32[]{:S(2)}) copy-start(bf16[2,512,256]{2,1,0:T(8,128)(2,1)} %constant.11.clone.refs_8_) | copy-start | bytes 1572868
  28.7 8.4 %collective-permute-start.7 = (f32[3,32,768]{2,1,0:T(8,128)S(1)}, f32[3,32,768]{2,1,0:T(8,128)S(1)}, u32[]{:S(2)}, u32[]{:S(2)}) collective-permute-start(f32[3,32,768]{2,1,0:T(8,128)S(1)} %shard_map.89), channel_id=1, source_target_pairs={{0,4},{4,0},{8,12},{12,8},{16,20},{20,16},{24,28},{28,24},{1,5},{5... | collective-permute-start | bytes 884744 | tf_op jit(solution)/shard_map/ppermute | solution.py:509
  28.7 5.5 %collective-permute-start.6 = (f32[32,768]{1,0:T(8,128)S(1)}, f32[32,768]{1,0:T(8,128)S(1)}, u32[]{:S(2)}, u32[]{:S(2)}) collective-permute-start(f32[32,768]{1,0:T(8,128)S(1)} %collective-permute-done.4.refs_1_), channel_id=1, source_target_pairs={{0,8},{4,12},{8,0},{12,4},{16,24},{20,28},{24,16},{28,20},{1,9},{5... | collective-permute-start | bytes 294920 | tf_op jit(solution)/shard_map/ppermute | solution.py:509
  29.0 4.0 %collective-permute-start.16 = (f32[32,768]{1,0:T(8,128)S(1)}, f32[32,768]{1,0:T(8,128)S(1)}, u32[]{:S(2)}, u32[]{:S(2)}) collective-permute-start(f32[32,768]{1,0:T(8,128)S(1)} %collective-permute-done.14.refs_3_), channel_id=1, source_target_pairs={{0,4},{4,0},{8,12},{12,8},{16,20},{20,16},{24,28},{28,24},{1,5},{5... | collective-permute-start | bytes 294920 | tf_op jit(solution)/shard_map/ppermute | solution.py:509
  29.3 1.2 %copy-start.7 = (bf16[4,2,256,256]{3,2,1,0:T(8,128)(2,1)S(1)}, bf16[4,2,256,256]{3,2,1,0:T(8,128)(2,1)}, u32[]{:S(2)}) copy-start(bf16[4,2,256,256]{3,2,1,0:T(8,128)(2,1)} %constant.9.clone.x_ref) | copy-start | bytes 3145732
  33.6 6.4 %collective-permute-start.17 = (f32[128,256]{1,0:T(8,128)S(1)}, f32[128,256]{1,0:T(8,128)S(1)}, u32[]{:S(2)}, u32[]{:S(2)}) collective-permute-start(f32[128,256]{1,0:T(8,128)S(1)} %get-tuple-element.29), channel_id=1, source_target_pairs={{0,1},{1,0},{2,3},{3,2},{4,5},{5,4},{6,7},{7,6},{8,9},{9,8},{10,11... | collective-permute-start | bytes 393224 | tf_op jit(solution)/shard_map/ppermute | solution.py:509
  34.2 3.0 %collective-permute-start.8 = (f32[32,768]{1,0:T(8,128)S(1)}, f32[32,768]{1,0:T(8,128)S(1)}, u32[]{:S(2)}, u32[]{:S(2)}) collective-permute-start(f32[32,768]{1,0:T(8,128)S(1)} %collective-permute-done.6.refs_3_), channel_id=1, source_target_pairs={{0,4},{4,0},{8,12},{12,8},{16,20},{20,16},{24,28},{28,24},{1,5},{5... | collective-permute-start | bytes 294920 | tf_op jit(solution)/shard_map/ppermute | solution.py:509
  34.2 10.8 %collective-permute-start.18 = (f32[128,256]{1,0:T(8,128)S(1)}, f32[128,256]{1,0:T(8,128)S(1)}, u32[]{:S(2)}, u32[]{:S(2)}) collective-permute-start(f32[128,256]{1,0:T(8,128)S(1)} %get-tuple-element.30), channel_id=1, source_target_pairs={{0,2},{1,3},{2,0},{3,1},{4,6},{5,7},{6,4},{7,5},{8,10},{9,11},{10,... | collective-permute-start | bytes 393224 | tf_op jit(solution)/shard_map/ppermute | solution.py:509
  35.7 9.3 %collective-permute-start.19 = (f32[128,256]{1,0:T(8,128)S(1)}, f32[128,256]{1,0:T(8,128)S(1)}, u32[]{:S(2)}, u32[]{:S(2)}) collective-permute-start(f32[128,256]{1,0:T(8,128)S(1)} %get-tuple-element.31), channel_id=1, source_target_pairs={{0,3},{1,2},{2,1},{3,0},{4,7},{5,6},{6,5},{7,4},{8,11},{9,10},{10,... | collective-permute-start | bytes 393224 | tf_op jit(solution)/shard_map/ppermute | solution.py:509
  37.1 7.9 %copy-start.3 = (bf16[2,256,512]{2,1,0:T(8,128)(2,1)S(1)}, bf16[2,256,512]{2,1,0:T(8,128)(2,1)}, u32[]{:S(2)}) copy-start(bf16[2,256,512]{2,1,0:T(8,128)(2,1)} %constant.8.clone.refs_6_) | copy-start | bytes 1572868
  37.1 7.8 %copy-start.4 = (f32[2,1,4,64,512]{4,3,2,1,0:T(8,128)S(1)}, f32[2,1,4,64,512]{4,3,2,1,0:T(8,128)}, u32[]{:S(2)}) copy-start(f32[2,1,4,64,512]{4,3,2,1,0:T(8,128)} %refs_5_.1) | copy-start | bytes 3145732
  37.6 10.9 %collective-permute-start.10 = (f32[128,256]{1,0:T(8,128)S(1)}, f32[128,256]{1,0:T(8,128)S(1)}, u32[]{:S(2)}, u32[]{:S(2)}) collective-permute-start(f32[128,256]{1,0:T(8,128)S(1)} %get-tuple-element.24), channel_id=1, source_target_pairs={{0,2},{1,3},{2,0},{3,1},{4,6},{5,7},{6,4},{7,5},{8,10},{9,11},{10,... | collective-permute-start | bytes 393224 | tf_op jit(solution)/shard_map/ppermute | solution.py:509
  39.2 9.3 %collective-permute-start.11 = (f32[128,256]{1,0:T(8,128)S(1)}, f32[128,256]{1,0:T(8,128)S(1)}, u32[]{:S(2)}, u32[]{:S(2)}) collective-permute-start(f32[128,256]{1,0:T(8,128)S(1)} %get-tuple-element.25), channel_id=1, source_target_pairs={{0,3},{1,2},{2,1},{3,0},{4,7},{5,6},{6,5},{7,4},{8,11},{9,10},{10,... | collective-permute-start | bytes 393224 | tf_op jit(solution)/shard_map/ppermute | solution.py:509
  39.9 8.6 %collective-permute-start.9 = (f32[128,256]{1,0:T(8,128)S(1)}, f32[128,256]{1,0:T(8,128)S(1)}, u32[]{:S(2)}, u32[]{:S(2)}) collective-permute-start(f32[128,256]{1,0:T(8,128)S(1)} %get-tuple-element.23), channel_id=1, source_target_pairs={{0,1},{1,0},{2,3},{3,2},{4,5},{5,4},{6,7},{7,6},{8,9},{9,8},{10,11... | collective-permute-start | bytes 393224 | tf_op jit(solution)/shard_map/ppermute | solution.py:509
where the time goes:
time: 51.2 us; the launch traced here: 50.9 us
  starting transfers between devices  20.7 us (40%)
  waiting for transfers between devices  18.5 us (36%)
  Pallas kernels  7.49 us (15%)
  local copies, waits for them, and re-layouts  3.46 us (7%)
  between operations  0.76 us (1%)
    ppermute x20, starting transfers between devices, exchange(): lax.ppermute(values, axis, [(index, index ^ mask) for index in range(size)])  20.7 us
    ppermute x20, waiting for transfers between devices, exchange(): lax.ppermute(values, axis, [(index, index ^ mask) for index in range(size)])  18.5 us
    pallas_call x9, Pallas kernels, call(): pl.pallas_call(kernel, out_shape=outs, in_specs=[pl.BlockSpec(memory_spac...  7.49 us
    unnamed x16, local copies, waits for them, and re-layouts  3.46 us
  transfers between devices with their start and end apart: 20, of which 7 were waited for; matrix products, arithmetic and copies ran while one was open for 0% of the time, Pallas kernels for 10%

commit v1 on v0

--- a/solution.py
+++ b/solution.py
@@ -176,6 +176,8 @@
 
 
 PEN = 4
+INV = 1
+PACK = (10**10, 0)
 HALF_ROWS = 32
 EXTRA = 8
 
@@ -199,20 +201,10 @@
     return np.sin(2.0 * np.pi / grid * (left * right % grid)) / math.sqrt(grid)
 
 
-def x_forward_table(grid):
+def x_table(grid):
     kx = np.arange(grid)
     x = kx[:, None]
     return split_table(np.concatenate([cosine(grid, x, kx), sine(grid, x, kx)], axis=1))
-
-
-def x_inverse_table(grid):
-    rows = grid // PEN
-    kx = np.arange(grid)[:, None]
-    tables = []
-    for device in range(PEN):
-        x = np.concatenate([block * rows + np.arange(rows) for block in (device, device ^ 2)])
-        tables.append(np.concatenate([cosine(grid, kx, x), sine(grid, kx, x)], axis=1))
-    return split_table(np.stack(tables))
 
 
 def row_numbers(device, rows):
@@ -229,7 +221,7 @@
         ky = row_numbers(device, rows)
         real = np.where(ky % (grid // 2) == 0, 1.0, 2.0) * cosine(grid, y, ky)
         imag = -2.0 * sine(grid, y, ky)
-        extra = (device ^ 2) * rows + HALF_ROWS
+        extra = (device ^ 1) * rows + HALF_ROWS
         far = (device ^ 3) * rows
         from_y = rows + HALF_ROWS
         extra_real, extra_imag = 2.0 * cosine(grid, y[:, 0], extra), -2.0 * sine(grid, y[:, 0], extra)
@@ -250,7 +242,7 @@
         ky = device * rows + np.arange(rows)[:, None]
         y = np.arange(grid)[None, :]
         parts += [cosine(grid, ky, y), -sine(grid, ky, y)]
-    return split_table(np.concatenate(parts, axis=0))
+    return split_table(np.concatenate([np.concatenate(parts[:4]), np.concatenate(parts[4:])], axis=1))
 
 
 def dot(left, right):
@@ -286,7 +278,7 @@
 
 
 def base_kernel(base_ref, own_ref, swap_ref):
-    mine = (lax.axis_index("pen") // 2) * 2
+    mine = (lax.axis_index("pen") % 2) * 2
     for out_ref, first in ((own_ref, mine), (swap_ref, 2 - mine)):
         for field in range(base_ref.shape[0]):
             out_ref[:, 128 * field : 128 * field + 128] = jnp.concatenate(
@@ -294,55 +286,41 @@
             )
 
 
-def state_kernel(state_ref, near_x_ref, near_y_ref, far_ref):
-    mine = (lax.axis_index("pen") // 2) * 2
-    far_ref[...] = jnp.zeros_like(far_ref)
-    near_y_ref[4 * HALF_ROWS :, :] = jnp.zeros((EXTRA, near_y_ref.shape[1]), jnp.float32)
-    for field in range(2):
-        for level in range(2):
-            index = 2 * field + level
-            place = slice(HALF_ROWS * index, HALF_ROWS * (index + 1))
-            near_x_ref[place, :] = state_ref[field, 0, mine + level, :HALF_ROWS, :]
-            other = 2 - mine + level
-            near_y_ref[place, :] = state_ref[field, 0, other, :HALF_ROWS, :]
-            line = slice(4 * HALF_ROWS + index, 4 * HALF_ROWS + index + 1)
-            near_y_ref[line, :] = state_ref[field, 0, other, HALF_ROWS : HALF_ROWS + 1, :]
-            far_ref[index : index + 1, :] = state_ref[field, 0, other, 0:1, :]
-
-
-def inverse_kernel(
-    grid, state_ref, near_x_ref, near_y_ref, far_ref, x_ref, y_ref, own_ref, swap_ref, held, mixed, high_ref, low_ref
-):
-    rows = state_ref.shape[3]
-    pen = lax.axis_index("pen")
-    mine = (pen // 2) * 2
-    odd = pen % 2 == 1
-    count = 2 * rows + EXTRA
-    for field in range(2):
-        for level in range(2):
-            index = 2 * field + level
-            place = slice(HALF_ROWS * index, HALF_ROWS * (index + 1))
-            held[index, :rows, :] = state_ref[field, 0, mine + level]
-            held[index, rows : rows + HALF_ROWS, :] = near_x_ref[place, :]
-            held[index, rows + HALF_ROWS : 2 * rows, :] = near_y_ref[place, :]
-            held[index, 2 * rows :, :] = jnp.zeros((EXTRA, 2 * grid), jnp.float32)
-            line = slice(4 * HALF_ROWS + index, 4 * HALF_ROWS + index + 1)
-            held[index, 2 * rows : 2 * rows + 1, :] = near_y_ref[line, :]
-            held[index, 2 * rows + 1 : 2 * rows + 2, :] = far_ref[index : index + 1, :]
-    row = lax.broadcasted_iota(jnp.int32, (count, 1), 0)
-    ky = jnp.where(
-        row < rows,
-        pen * rows + row,
-        jnp.where(
-            row < rows + HALF_ROWS,
-            (pen ^ 1) * rows + row - rows,
-            jnp.where(
-                row <= 2 * rows, (pen ^ 2) * rows + row - rows - HALF_ROWS, (pen ^ 3) * rows
-            ),
-        ),
-    )
+def lines_kernel(block_ref, state_ref, out_ref):
+    other = 2 - (lax.axis_index("pen") % 2) * 2
+    tall = block_ref.shape[0]
+    out_ref[:tall, :] = block_ref[...]
+    out_ref[tall:, :] = jnp.zeros((EXTRA, out_ref.shape[1]), jnp.float32)
+    for index in range(4):
+        out_ref[tall + index : tall + index + 1, : state_ref.shape[4]] = state_ref[
+            index // 2, 0, other + index % 2, 0:1, :
+        ]
+
+
+def near_x_kernel(state_ref, near_ref):
+    other = 2 - (lax.axis_index("pen") % 2) * 2
+    near_ref[4 * HALF_ROWS :, :] = jnp.zeros((EXTRA, near_ref.shape[1]), jnp.float32)
+    for index in range(4):
+        rows = state_ref[index // 2, 0, other + index % 2, : HALF_ROWS + EXTRA, :]
+        near_ref[HALF_ROWS * index : HALF_ROWS * (index + 1), :] = rows[:HALF_ROWS]
+        line = 4 * HALF_ROWS + index
+        near_ref[line : line + 1, :] = rows[HALF_ROWS : HALF_ROWS + 1]
+
+
+def relay_kernel(came_ref, state_ref, swap_ref, near_ref):
+    mine = (lax.axis_index("pen") % 2) * 2
+    tall = swap_ref.shape[0]
+    swap_ref[...] = came_ref[:tall, :]
+    near_ref[4 * HALF_ROWS :, :] = came_ref[tall:, : near_ref.shape[1]]
+    for index in range(4):
+        near_ref[HALF_ROWS * index : HALF_ROWS * (index + 1), :] = state_ref[
+            index // 2, 0, mine + index % 2, :HALF_ROWS, :
+        ]
+
+
+def x_stage(grid, table, ky, held):
+    count = held[0].shape[0]
     kappa_y, kappa_x, _, inverse = wave_arrays(ky, grid)
-    table = (x_ref[pen, 0], x_ref[pen, 1])
     fields = [
         (0, inverse, kappa_y),
         (0, -kappa_x * inverse, None),
@@ -351,53 +329,111 @@
         (1, kappa_x, None),
         (1, None, kappa_y),
     ]
-    for number, (field, before, after) in enumerate(fields):
+    for field, before, after in fields:
         stacked = []
         for level in range(2):
             for columns in (slice(0, grid), slice(grid, 2 * grid)):
-                values = held[2 * field + level, :, columns]
+                values = held[2 * field + level][:, columns]
                 stacked.append(values if before is None else values * before)
         product = dot_split(split(jnp.concatenate(stacked, axis=0)), table)
+        results = []
         for level in range(2):
             top = product[2 * level * count : (2 * level + 1) * count]
             bottom = product[(2 * level + 1) * count : (2 * level + 2) * count]
             real = -(bottom[:, :128] + top[:, 128:])
             imag = top[:, :128] - bottom[:, 128:]
-            if after is not None:
-                real, imag = after * real, after * imag
-            mixed[level, : 2 * rows, :] = real[: 2 * rows]
-            mixed[level, 2 * rows :, :] = imag[: 2 * rows]
-            extra_real, extra_imag = real[2 * rows : 2 * rows + 1], imag[2 * rows : 2 * rows + 1]
-            far_real = real[2 * rows + 1 : 2 * rows + 2]
-            from_y = rows + HALF_ROWS
+            results.append((real, imag) if after is None else (after * real, after * imag))
+        yield results
+
+
+def x_columns(grid, x_ref):
+    start = pl.multiple_of((lax.axis_index("pen") // 2) * 128, 128)
+    return [
+        jnp.concatenate(
+            [x_ref[part, :, pl.ds(start, 128)], x_ref[part, :, pl.ds(grid + start, 128)]], axis=1
+        )
+        for part in range(2)
+    ]
+
+
+def own_rows_kernel(grid, state_ref, x_ref, real_ref, imag_ref):
+    rows = state_ref.shape[3]
+    pen = lax.axis_index("pen")
+    mine = (pen % 2) * 2
+    held = [state_ref[field, 0, mine + level] for field in range(2) for level in range(2)]
+    ky = pen * rows + lax.broadcasted_iota(jnp.int32, (rows, 1), 0)
+    for number, results in enumerate(x_stage(grid, x_columns(grid, x_ref), ky, held)):
+        for level, (real, imag) in enumerate(results):
+            real_ref[level, number] = real
+            imag_ref[level, number] = imag
+
+
+def inverse_kernel(
+    grid, near_x_ref, near_y_ref, own_real, own_imag, x_ref, y_ref, own_ref, swap_ref, mixed, high_ref, low_ref, y_held, sem
+):
+    y_copy = pltpu.make_async_copy(y_ref.at[lax.axis_index("pen")], y_held, sem)
+    y_copy.start()
+    rows = own_real.shape[2]
+    pen = lax.axis_index("pen")
+    odd = pen % 2 == 1
+    count = rows + EXTRA
+    held = []
+    for index in range(4):
+        place = slice(HALF_ROWS * index, HALF_ROWS * (index + 1))
+        line = slice(4 * HALF_ROWS + index, 4 * HALF_ROWS + index + 1)
+        held.append(
+            jnp.concatenate(
+                [
+                    near_x_ref[place, :],
+                    near_y_ref[place, :],
+                    near_x_ref[line, :],
+                    near_y_ref[line, :],
+                    jnp.zeros((EXTRA - 2, 2 * grid), jnp.float32),
+                ],
+                axis=0,
+            )
+        )
+    row = lax.broadcasted_iota(jnp.int32, (count, 1), 0)
+    ky = jnp.where(row < HALF_ROWS, (pen ^ 1) * rows + row, (pen ^ 2) * rows + row - HALF_ROWS)
+    ky = jnp.where(row == rows, (pen ^ 1) * rows + HALF_ROWS, ky)
+    ky = jnp.where(row > rows, (pen ^ 3) * rows, ky)
+    from_y = rows + HALF_ROWS
+    for number, results in enumerate(x_stage(grid, x_columns(grid, x_ref), ky, held)):
+        for level, (real, imag) in enumerate(results):
+            first_imag = own_imag[level, number, 0:1, :]
+            mixed[level, :rows, :] = own_real[level, number]
+            mixed[level, rows : 2 * rows, :] = real[:rows]
+            mixed[level, 2 * rows : 3 * rows, :] = own_imag[level, number]
+            mixed[level, 3 * rows :, :] = imag[:rows]
+            extra_real, extra_imag = real[rows : rows + 1], imag[rows : rows + 1]
+            far_real = real[rows + 1 : rows + 2]
             mixed[level, from_y : from_y + 1, :] = jnp.where(
-                odd, extra_real, real[from_y : from_y + 1]
-            )
-            mixed[level, 2 * rows : 2 * rows + 1, :] = jnp.where(odd, imag[0:1], extra_real)
-            mixed[level, 3 * rows : 3 * rows + 1, :] = jnp.where(
-                odd, far_real, imag[rows : rows + 1]
-            )
+                odd, extra_real, real[HALF_ROWS : HALF_ROWS + 1]
+            )
+            mixed[level, 2 * rows : 2 * rows + 1, :] = jnp.where(odd, first_imag, extra_real)
+            mixed[level, 3 * rows : 3 * rows + 1, :] = jnp.where(odd, far_real, imag[0:1])
             mixed[level, 2 * rows + from_y : 2 * rows + from_y + 1, :] = extra_imag
         for block, values in enumerate(interleave(mixed[0], mixed[1])):
             high, low = split(values)
-            high_ref[block, :, 128 * number : 128 * number + 128] = high
-            low_ref[block, :, 128 * number : 128 * number + 128] = low
-    left = (y_ref[pen, 0], y_ref[pen, 1])
+            high_ref[block ^ (pen % 2), :, 128 * number : 128 * number + 128] = high
+            low_ref[block ^ (pen % 2), :, 128 * number : 128 * number + 128] = low
+    y_copy.wait()
+    left = (y_held[0], y_held[1])
     own_ref[...] = dot_split(left, (high_ref[0], low_ref[0]))
     swap_ref[...] = dot_split(left, (high_ref[1], low_ref[1]))
 
 
-def advection_kernel(masks, rows, field_ref, *refs):
-    blocks, forward_ref = refs[: len(masks)], refs[len(masks)]
-    outs, (high_ref, low_ref) = refs[len(masks) + 1 : len(masks) + 1 + PEN], refs[-2:]
+def advection_kernel(offsets, rows, field_ref, *refs):
+    packs, table_ref = refs[:2], refs[2]
+    outs, (high_ref, low_ref) = refs[3 : 3 + PEN], refs[-2:]
     ens = lax.axis_index("ens")
-    for (mask, slot), block in zip(masks, blocks, strict=True):
-        tall = block.shape[-2]
+    tall = packs[0].shape[0] // len(offsets)
+    for which, slot in [(which, slot) for which in range(2) for slot in range(len(offsets))]:
+        mask = offsets[slot] ^ which
         place = pl.ds(pl.multiple_of((ens ^ mask) * tall, tall), tall)
 
-        def base(index, block=block, slot=slot):
-            lanes = slice(128 * index, 128 * index + 128)
-            return block[:, lanes] if slot is None else block[slot, :, lanes]
+        def base(index, which=which, slot=slot):
+            return packs[which][tall * slot : tall * (slot + 1), 128 * index : 128 * index + 128]
 
         def field(index, place=place):
             return field_ref[place, 128 * index : 128 * index + 128]
@@ -413,10 +449,13 @@
             high_ref[place, 128 * output : 128 * output + 128] = high
             low_ref[place, 128 * output : 128 * output + 128] = low
     pen = lax.axis_index("pen")
+    grid = table_ref.shape[1]
     for step in range(PEN):
-        place = pl.ds(pl.multiple_of((pen ^ step) * 2 * rows, 2 * rows), 2 * rows)
+        target = pen ^ step
+        place = pl.ds(pl.multiple_of((target % 2) * 2 * rows, 2 * rows), 2 * rows)
+        lanes = pl.ds(pl.multiple_of((target // 2) * grid, grid), grid)
         outs[step][...] = dot_split(
-            (forward_ref[0, place, :], forward_ref[1, place, :]), (high_ref[...], low_ref[...])
+            (table_ref[2, place, lanes], table_ref[3, place, lanes]), (high_ref[...], low_ref[...])
         )
 
 
@@ -426,15 +465,19 @@
         gathered[pen ^ step] = messages[step][...]
     grid = table_ref.shape[1]
     for pair in range(2):
-        block = pair if chunk == 0 else 1 - pair
-        lines = slice(2 * rows * block, 2 * rows * (block + 1))
+        first = (pair if chunk == 0 else 1 - pair) * rows
+        table = [
+            jnp.concatenate(
+                [table_ref[part, first : first + rows, :], table_ref[part, first + 2 * rows : first + 3 * rows, :]],
+                axis=0,
+            )
+            for part in range(2)
+        ]
         stacked = []
         for field in range(2):
             lanes = slice(128 * field, 128 * field + 128)
-            stacked += interleave(gathered[2 * pair, :, lanes], gathered[2 * pair + 1, :, lanes])
-        product = dot_split(
-            split(jnp.concatenate(stacked, axis=0)), (table_ref[0, lines, :], table_ref[1, lines, :])
-        )
+            stacked += interleave(gathered[pair, :, lanes], gathered[pair + 2, :, lanes])
+        product = dot_split(split(jnp.concatenate(stacked, axis=0)), table)
         for index in range(4):
             top = product[2 * index * rows : (2 * index + 1) * rows]
             bottom = product[(2 * index + 1) * rows : (2 * index + 2) * rows]
@@ -476,123 +519,120 @@
 
 
 def second_kernel(grid, *refs):
-    messages, (state_ref, part_ref, table_ref, state_out, accum_out, gathered) = refs[:PEN], refs[PEN:]
+    messages = refs[:PEN]
+    state_ref, part_ref, table_ref, state_out, accum_out, gathered, state_next, accum_next, sems = refs[PEN:]
     rows = state_ref.shape[3]
+    copies = []
     for field, level, *advect in x_forward(1, messages, gathered, table_ref, rows):
         for columns, values in zip((slice(0, grid), slice(grid, 2 * grid)), advect, strict=True):
             memory = part_ref[field, 0, level, :, columns] - values
-            accum_out[field, 0, level, :, columns] = memory
-            state_out[field, 0, level, :, columns] = (
+            accum_next[field, 0, level, :, columns] = memory
+            state_next[field, 0, level, :, columns] = (
                 state_ref[field, 0, level, :, columns] + weight_factor * time_step * memory
             )
+        for which, (held, out) in enumerate(((state_next, state_out), (accum_next, accum_out))):
+            copy = pltpu.make_async_copy(
+                held.at[field, 0, level], out.at[field, 0, level], sems.at[which, field, level]
+            )
+            copy.start()
+            copies.append(copy)
+    for copy in copies:
+        copy.wait()
 
 
 def pack_kernel(*refs):
-    for index, ref in enumerate(refs[:-1]):
-        refs[-1][index] = ref[...]
-
-
-def call(kernel, outs, scratch, flops, args, limit=40):
-    total = sum(math.prod(a.shape) * a.dtype.itemsize for a in list(args) + list(outs))
+    tall = refs[0].shape[0]
+    for slot, ref in enumerate(refs[:-1]):
+        refs[-1][tall * slot : tall * (slot + 1), :] = ref[...]
+
+
+def call(kernel, outs, scratch, cost, args, outside=(), outs_outside=False, after=(), limit=24):
+    args, after = list(args), list(after)
+    spaces = [pltpu.HBM if index in outside else pltpu.VMEM for index in range(len(args))]
+    spaces += [pl.ANY] * len(after)
+    count = len(args)
+    total = sum(math.prod(a.shape) * a.dtype.itemsize for a in args + list(outs))
     return pl.pallas_call(
-        kernel,
+        lambda *refs: kernel(*refs[:count], *refs[count + len(after) :]),
         out_shape=outs,
-        in_specs=[pl.BlockSpec(memory_space=pltpu.VMEM)] * len(args),
-        out_specs=[pl.BlockSpec(memory_space=pltpu.VMEM)] * len(outs),
+        in_specs=[pl.BlockSpec(memory_space=space) for space in spaces],
+        out_specs=[pl.BlockSpec(memory_space=pltpu.HBM if outs_outside else pltpu.VMEM)] * len(outs),
         scratch_shapes=scratch,
         compiler_params=pltpu.CompilerParams(vmem_limit_bytes=limit * 1024 * 1024),
-        cost_estimate=pl.CostEstimate(flops=flops, bytes_accessed=total, transcendentals=0),
-    )(*args)
+        cost_estimate=pl.CostEstimate(flops=cost, bytes_accessed=total, transcendentals=0),
+        name=getattr(kernel, "func", kernel).__name__,
+    )(*args, *after)
 
 
 def exchange(values, axis, size, mask):
     return lax.ppermute(values, axis, [(index, index ^ mask) for index in range(size)])
 
 
-def gather_blocks(block, size):
-    held = {0: block}
-    bit = size // 2
-    while bit > 1:
-        for offset in list(held):
-            mask = 2 * bit - 2
-            held[offset ^ mask] = exchange(held[offset], "ens", size, mask)
-        bit //= 2
-    offsets = list(held)
-    early, last = offsets[:-1], offsets[-1]
-    shape = jax.ShapeDtypeStruct((len(early),) + block.shape, block.dtype)
-    (packed,) = call(pack_kernel, [shape], [], 0, [held[offset] for offset in early])
-    packed = exchange(packed, "ens", size, 1)
-    final = exchange(held[last], "ens", size, 1)
-    found = [((offset, None), held[offset]) for offset in offsets]
-    found += [((offset ^ 1, slot), packed) for slot, offset in enumerate(early)]
-    found.append(((last ^ 1, None), final))
+def gather_blocks(blocks, size, after):
+    found = []
+    for block, wait, cost in zip(blocks, after, PACK, strict=True):
+        held = {0: block}
+        bit = size // 2
+        while bit > 1:
+            for offset, array in list(held.items()):
+                held[offset ^ (2 * bit - 2)] = exchange(array, "ens", size, 2 * bit - 2)
+            bit //= 2
+        shape = jax.ShapeDtypeStruct((len(held) * block.shape[0], block.shape[1]), block.dtype)
+        (packed,) = call(pack_kernel, [shape], [], cost, list(held.values()), after=wait)
+        found.append((tuple(held), packed, exchange(packed, "ens", size, 1)))
     return found
 
 
 def on_device(axes, state, accum, base_flow):
     grid, rows, levels = state.shape[-1] // 2, state.shape[3], state.shape[2]
     size = axes["ens"]
-    if axes["pen"] != PEN or levels != 4 or grid != 256 or size & (size - 1):
+    if axes["pen"] != PEN or levels != 4 or grid != 256 or size < 4 or size & (size - 1):
         return on_device_general(state, accum, base_flow)
     f32, bf16 = jnp.float32, jnp.bfloat16
     shape = functools.partial(jax.ShapeDtypeStruct, dtype=f32)
     fields, _, wide, tall = base_flow.shape
     lanes = 2 * wide
-    x_forward_parts = jnp.asarray(x_forward_table(grid))
-
-    own_base, swap_base = call(
-        base_kernel,
-        [shape((tall, fields * lanes))] * 2,
+    table = jnp.asarray(np.concatenate([x_table(grid), y_forward_table(grid)]))
+    y_table = y_inverse_table(grid)
+    base_lanes = fields * lanes
+    block, message = shape((tall, base_lanes)), shape((4 * HALF_ROWS + EXTRA, 2 * grid))
+    own_base, swap_base = call(base_kernel, [block] * 2, [], 0, [jnp.swapaxes(base_flow, 2, 3)])
+    (swap_base,) = call(lines_kernel, [shape((tall + EXTRA, base_lanes))], [], 0, [swap_base, state])
+    came = exchange(swap_base, "pen", PEN, 1)
+    (near_x,) = call(near_x_kernel, [message], [], 0, [state], after=[swap_base])
+    near_x = exchange(near_x, "pen", PEN, 1)
+    swap_base, near_y = call(relay_kernel, [block, message], [], 0, [came, state])
+    near_y = exchange(near_y, "pen", PEN, 2)
+    own_parts = call(
+        functools.partial(own_rows_kernel, grid),
+        [shape((2, fields, rows, lanes))] * 2,
         [],
-        0,
-        [jnp.swapaxes(base_flow, 2, 3)],
-    )
-    own_blocks = gather_blocks(own_base, size)
-    swap_blocks = gather_blocks(exchange(swap_base, "pen", PEN, 2), size)
-    near_x, near_y, far = call(
-        state_kernel,
-        [
-            shape((4 * HALF_ROWS, 2 * grid)),
-            shape((4 * HALF_ROWS + EXTRA, 2 * grid)),
-            shape((EXTRA, 2 * grid)),
-        ],
-        [],
-        0,
-        [state],
-    )
-    near_x = exchange(near_x, "pen", PEN, 1)
-    near_y = exchange(near_y, "pen", PEN, 2)
-    far = exchange(far, "pen", PEN, 3)
-    count = 2 * rows + EXTRA
+        6 * fields * 4 * rows * grid * 256,
+        [state, table],
+    )
     own_fields, swap_fields = call(
         functools.partial(inverse_kernel, grid),
-        [shape((grid, fields * lanes))] * 2,
+        [shape((grid, base_lanes))] * 2,
         [
-            pltpu.VMEM((4, count, 2 * grid), f32),
             pltpu.VMEM((2, 4 * rows, lanes), f32),
-            pltpu.VMEM((2, grid, fields * lanes), bf16),
-            pltpu.VMEM((2, grid, fields * lanes), bf16),
+            pltpu.VMEM((2, grid, base_lanes), bf16),
+            pltpu.VMEM((2, grid, base_lanes), bf16),
+            pltpu.VMEM(y_table.shape[1:], bf16),
+            pltpu.SemaphoreType.DMA,
         ],
-        6 * fields * 4 * count * grid * 256 + 12 * grid * grid * fields * lanes,
-        [
-            state,
-            near_x,
-            near_y,
-            far,
-            jnp.asarray(x_inverse_table(grid)),
-            jnp.asarray(y_inverse_table(grid)),
-        ],
-    )
+        INV * (6 * fields * 4 * (rows + EXTRA) * grid * 256 + 12 * grid * grid * base_lanes),
+        [near_x, near_y, *own_parts, table, jnp.asarray(y_table)],
+        outside=(5,),
+    )
+    blocks = gather_blocks((own_base, swap_base), size, ((), (own_fields,)))
     back = []
-    forward = jnp.asarray(y_forward_table(grid))
-    for physical, blocks in ((own_fields, own_blocks), (swap_fields, swap_blocks)):
-        masks = tuple(key for key, _ in blocks)
+    for physical, (offsets, packed, partner) in zip((own_fields, swap_fields), blocks, strict=True):
         parts = call(
-            functools.partial(advection_kernel, masks, rows),
+            functools.partial(advection_kernel, offsets, rows),
             [shape((2 * rows, 2 * lanes))] * PEN,
             [pltpu.VMEM((grid, 2 * lanes), bf16)] * 2,
             6 * 2 * grid * grid * 2 * lanes,
-            [physical] + [block for _, block in blocks] + [forward],
+            [physical, packed, partner, table],
         )
         back.append([parts[0]] + [exchange(parts[step], "pen", PEN, step) for step in range(1, PEN)])
     gathered = [pltpu.VMEM((PEN, 2 * rows, 2 * lanes), f32)]
@@ -602,14 +642,17 @@
         [shape(state.shape)],
         gathered,
         flops,
-        back[0] + [state, accum, x_forward_parts],
+        back[0] + [state, accum, table],
     )
     state_next, accum_next = call(
         functools.partial(second_kernel, grid),
         [shape(state.shape), shape(state.shape)],
-        gathered,
+        gathered
+        + [pltpu.VMEM(state.shape, f32)] * 2
+        + [pltpu.SemaphoreType.DMA((2, 2, levels))],
         flops,
-        back[1] + [state, part, x_forward_parts],
+        back[1] + [state, part, table],
+        outs_outside=True,
     )
     return state_next, accum_next
 

time: 51.2 us -> 44.6 us (0.87)
  waiting for transfers between devices: 18.5 us -> 10.2 us
  starting transfers between devices: 20.7 us -> 23.1 us
  local copies, waits for them, and re-layouts: 3.46 us -> 2.23 us
  Pallas kernels: 7.49 us -> 8.14 us
    ppermute x20 -> x17, waiting for transfers between devices: 18.5 us -> 10.2 us  [exchange(): lax.ppermute(values, axis, [(index, index ^ mask) for index in range(size)])]
    ppermute x20 -> x17, starting transfers between devices: 20.7 us -> 23.1 us  [exchange(): lax.ppermute(values, axis, [(index, index ^ mask) for index in range(size)])]
    unnamed x16 -> x12, local copies, waits for them, and re-layouts: 3.46 us -> 2.23 us
    pallas_call x9 -> x12, Pallas kernels: 7.49 us -> 8.14 us  [call(): pl.pallas_call(lambda *refs: kernel(*refs[:count], *refs[count + len(afte...]
  transfers between devices with their start and end apart: 20 -> 17, of which waited for: 7 -> 7; matrix products, arithmetic and copies ran while one was open for 0% -> 0% of each run, Pallas kernels for 10% -> 13%
where the time goes in v1:
time: 44.6 us; the launch traced here: 44.4 us
  starting transfers between devices  23.1 us (52%)
  waiting for transfers between devices  10.2 us (23%)
  Pallas kernels  8.14 us (18%)
  local copies, waits for them, and re-layouts  2.23 us (5%)
  between operations  0.77 us (2%)
    ppermute x17, starting transfers between devices, exchange(): lax.ppermute(values, axis, [(index, index ^ mask) for index in range(size)])  23.1 us
    ppermute x17, waiting for transfers between devices, exchange(): lax.ppermute(values, axis, [(index, index ^ mask) for index in range(size)])  10.2 us
    pallas_call x12, Pallas kernels, call(): pl.pallas_call(lambda *refs: kernel(*refs[:count], *refs[count + len(afte...  8.14 us
    unnamed x12, local copies, waits for them, and re-layouts  2.23 us
  transfers between devices with their start and end apart: 17, of which 7 were waited for; matrix products, arithmetic and copies ran while one was open for 0% of the time, Pallas kernels for 13%

profile of v1, /device:TPU:0, one launch (start us, length us, event | category | flops | bytes accessed | tf_op | source)
XLA Modules:
  0.0 44.4 jit_solution(14774703051734916414)
XLA Ops:
  0.6 0.0 copy-start.4
  0.6 1.0 %copy-done.4 = f32[6,4,64,32]{2,3,1,0:T(8,128)S(1)} copy-done((f32[6,4,64,32]{2,3,1,0:T(8,128)S(1)}, f32[6,4,64,32]{2,3,1,0:T(8,128)}, u32[]{:S(2)}) %copy-start.4) | copy-done | bytes 196632
  1.6 0.1 base_kernel.1
  1.7 5.1 %collective-permute-start.10 = (f32[32,768]{1,0:T(8,128)S(1)}, f32[32,768]{1,0:T(8,128)S(1)}, u32[]{:S(2)}, u32[]{:S(2)}) collective-permute-start(f32[32,768]{1,0:T(8,128)S(1)} %get-tuple-element.29.refs_0_), channel_id=1, source_target_pairs={{0,24},{4,28},{8,16},{12,20},{16,8},{20,12},{24,0},{28,4},{1,25},{... | collective-permute-start | bytes 294920 | tf_op jit(solution)/shard_map/ppermute | solution.py:568
  6.9 0.0 copy-start
  6.9 1.2 %copy-done = f32[2,1,4,64,512]{4,3,2,1,0:T(8,128)S(1)} copy-done((f32[2,1,4,64,512]{4,3,2,1,0:T(8,128)S(1)}, f32[2,1,4,64,512]{4,3,2,1,0:T(8,128)}, u32[]{:S(2)}) %copy-start) | copy-done | bytes 1048600
  8.1 0.0 copy-start.1
  8.1 1.6 %collective-permute-start.1 = (f32[40,768]{1,0:T(8,128)S(1)}, f32[40,768]{1,0:T(8,128)S(1)}, u32[]{:S(2)}, u32[]{:S(2)}) collective-permute-start(f32[40,768]{1,0:T(8,128)S(1)} %lines_kernel.1.refs_1_), channel_id=1, source_target_pairs={{0,1},{1,0},{2,3},{3,2},{4,5},{5,4},{6,7},{7,6},{8,9},{9,8},{10,11... | collective-permute-start | bytes 368648 | tf_op jit(solution)/shard_map/ppermute | solution.py:568
  9.7 0.0 collective-permute-start.11
  9.7 0.1 collective-permute-done.10.refs_1_
  9.8 1.9 %collective-permute-start.12 = (f32[32,768]{1,0:T(8,128)S(1)}, f32[32,768]{1,0:T(8,128)S(1)}, u32[]{:S(2)}, u32[]{:S(2)}) collective-permute-start(f32[32,768]{1,0:T(8,128)S(1)} %collective-permute-done.10.refs_1_), channel_id=1, source_target_pairs={{0,8},{4,12},{8,0},{12,4},{16,24},{20,28},{24,16},{28,20},{1,9},{5... | collective-permute-start | bytes 294920 | tf_op jit(solution)/shard_map/ppermute | solution.py:568
  11.7 0.0 copy-done.1
  11.7 1.3 %collective-permute-start = (f32[136,512]{1,0:T(8,128)S(1)}, f32[136,512]{1,0:T(8,128)S(1)}, u32[]{:S(2)}, u32[]{:S(2)}) collective-permute-start(f32[136,512]{1,0:T(8,128)S(1)} %near_x_kernel.1), channel_id=1, source_target_pairs={{0,1},{1,0},{2,3},{3,2},{4,5},{5,4},{6,7},{7,6},{8,9},{9,8},{10,11... | collective-permute-start | bytes 835592 | tf_op jit(solution)/shard_map/ppermute | solution.py:568
  13.1 0.0 collective-permute-done.1.refs_0_
  13.1 1.6 %collective-permute-start.2 = (f32[136,512]{1,0:T(8,128)S(1)}, f32[136,512]{1,0:T(8,128)S(1)}, u32[]{:S(2)}, u32[]{:S(2)}) collective-permute-start(f32[136,512]{1,0:T(8,128)S(1)} %get-tuple-element.19), channel_id=1, source_target_pairs={{0,2},{1,3},{2,0},{3,1},{4,6},{5,7},{6,4},{7,5},{8,10},{9,11},{10,... | collective-permute-start | bytes 835592 | tf_op jit(solution)/shard_map/ppermute | solution.py:568
  14.7 0.0 copy-start.2
  14.7 2.5 %collective-permute-start.3 = (f32[32,768]{1,0:T(8,128)S(1)}, f32[32,768]{1,0:T(8,128)S(1)}, u32[]{:S(2)}, u32[]{:S(2)}) collective-permute-start(f32[32,768]{1,0:T(8,128)S(1)} %get-tuple-element.23.refs_0_), channel_id=1, source_target_pairs={{0,24},{4,28},{8,16},{12,20},{16,8},{20,12},{24,0},{28,4},{1,25},{... | collective-permute-start | bytes 294920 | tf_op jit(solution)/shard_map/ppermute | solution.py:568
  17.2 0.0 collective-permute-done.11.refs_2_
  17.2 0.0 collective-permute-done.12.refs_3_
  17.2 0.0 copy-start.5
  17.2 0.1 collective-permute-start.13
  17.3 0.0 copy-done.2
  17.3 0.8 %own_rows_kernel.1 = (f32[2,6,64,128]{3,2,1,0:T(8,128)S(1)}, f32[2,6,64,128]{3,2,1,0:T(8,128)S(1)}) custom-call(f32[2,1,4,64,512]{4,3,2,1,0:T(8,128)S(1)} %copy-done.1, bf16[4,256,512]{2,1,0:T(8,128)(2,1)S(1)} %copy-done.2), custom_call_target="tpu_custom_call" | custom-call | flops 603979776 | bytes 2883584 | tf_op jit(solution)/shard_map/own_rows_kernel/pallas_call | solution.py:555
  18.2 1.2 %collective-permute-start.4 = (f32[32,768]{1,0:T(8,128)S(1)}, f32[32,768]{1,0:T(8,128)S(1)}, u32[]{:S(2)}, u32[]{:S(2)}) collective-permute-start(f32[32,768]{1,0:T(8,128)S(1)} %get-tuple-element.23.refs_0_), channel_id=1, source_target_pairs={{0,8},{4,12},{8,0},{12,4},{16,24},{20,28},{24,16},{28,20},{1,9},{5... | collective-permute-start | bytes 294920 | tf_op jit(solution)/shard_map/ppermute | solution.py:568
  19.4 1.8 %collective-permute-done.3.refs_1_ = f32[32,768]{1,0:T(8,128)S(1)} collective-permute-done((f32[32,768]{1,0:T(8,128)S(1)}, f32[32,768]{1,0:T(8,128)S(1)}, u32[]{:S(2)}, u32[]{:S(2)}) %collective-permute-start.3) | collective-permute-done | bytes 98336 | tf_op jit(solution)/shard_map/ppermute | solution.py:568
  21.2 0.8 %collective-permute-start.5 = (f32[32,768]{1,0:T(8,128)S(1)}, f32[32,768]{1,0:T(8,128)S(1)}, u32[]{:S(2)}, u32[]{:S(2)}) collective-permute-start(f32[32,768]{1,0:T(8,128)S(1)} %collective-permute-done.3.refs_1_), channel_id=1, source_target_pairs={{0,8},{4,12},{8,0},{12,4},{16,24},{20,28},{24,16},{28,20},{1,9},{5... | collective-permute-start | bytes 294920 | tf_op jit(solution)/shard_map/ppermute | solution.py:568
  22.0 0.0 collective-permute-done.refs_0_
  22.0 0.0 collective-permute-done.2.refs_1_
  22.0 0.0 copy-done.5
  22.0 2.3 %inverse_kernel.1 = (f32[256,768]{1,0:T(8,128)S(1)}, f32[256,768]{1,0:T(8,128)S(1)}) custom-call(f32[136,512]{1,0:T(8,128)S(1)} %collective-permute-done.refs_0_, f32[136,512]{1,0:T(8,128)S(1)} %collective-permute-done.2.refs_1_, f32[2,6,64,128]{3,2,1,0:T(8,128)S(1)} %get-tuple-element.20.refs_2_, f32[2,6,64,128]{3,2,1,0:T(8,128)S(1)} %get-tuple-element.21.refs_3_, ...), custom_call_target="tpu_custom_call" | custom-call | flops 1283457024 | bytes 5013504 | tf_op jit(solution)/shard_map/inverse_kernel/pallas_call | solution.py:555
  24.3 0.0 collective-permute-done.4.refs_2_
  24.3 1.5 %collective-permute-done.5.refs_3_ = f32[32,768]{1,0:T(8,128)S(1)} collective-permute-done((f32[32,768]{1,0:T(8,128)S(1)}, f32[32,768]{1,0:T(8,128)S(1)}, u32[]{:S(2)}, u32[]{:S(2)}) %collective-permute-start.5) | collective-permute-done | bytes 98336 | tf_op jit(solution)/shard_map/ppermute | solution.py:568
  25.9 0.1 collective-permute-start.6
  25.9 0.0 collective-permute-done.13.refs_2_
  25.9 0.5 %advection_kernel.3 = (f32[128,256]{1,0:T(8,128)S(1)}, f32[128,256]{1,0:T(8,128)S(1)}, f32[128,256]{1,0:T(8,128)S(1)}, f32[128,256]{1,0:T(8,128)S(1)}) custom-call(f32[256,768]{1,0:T(8,128)S(1)} %get-tuple-element.24.refs_4_.refs_0_, f32[128,768]{1,0:T(8,128)S(1)} %pack_kernel.3.refs_1_, f32[128,768]{1,0:T(8,128)S(1)} %collective-permute-done.13.refs_2_, ...), custom_call_target="tpu_custom_call" | custom-call | flops 201326592 | bytes 3145728 | tf_op jit(solution)/shard_map/advection_kernel/pallas_call | solution.py:555
  26.4 1.5 %collective-permute-start.14 = (f32[128,256]{1,0:T(8,128)S(1)}, f32[128,256]{1,0:T(8,128)S(1)}, u32[]{:S(2)}, u32[]{:S(2)}) collective-permute-start(f32[128,256]{1,0:T(8,128)S(1)} %get-tuple-element.31), channel_id=1, source_target_pairs={{0,1},{1,0},{2,3},{3,2},{4,5},{5,4},{6,7},{7,6},{8,9},{9,8},{10,11... | collective-permute-start | bytes 393224 | tf_op jit(solution)/shard_map/ppermute | solution.py:568
  28.0 0.5 %collective-permute-start.15 = (f32[128,256]{1,0:T(8,128)S(1)}, f32[128,256]{1,0:T(8,128)S(1)}, u32[]{:S(2)}, u32[]{:S(2)}) collective-permute-start(f32[128,256]{1,0:T(8,128)S(1)} %get-tuple-element.32), channel_id=1, source_target_pairs={{0,2},{1,3},{2,0},{3,1},{4,6},{5,7},{6,4},{7,5},{8,10},{9,11},{10,... | collective-permute-start | bytes 393224 | tf_op jit(solution)/shard_map/ppermute | solution.py:568
  28.5 1.5 %collective-permute-start.16 = (f32[128,256]{1,0:T(8,128)S(1)}, f32[128,256]{1,0:T(8,128)S(1)}, u32[]{:S(2)}, u32[]{:S(2)}) collective-permute-start(f32[128,256]{1,0:T(8,128)S(1)} %get-tuple-element.33), channel_id=1, source_target_pairs={{0,3},{1,2},{2,1},{3,0},{4,7},{5,6},{6,5},{7,4},{8,11},{9,10},{10,... | collective-permute-start | bytes 393224 | tf_op jit(solution)/shard_map/ppermute | solution.py:568
  30.0 0.0 collective-permute-done.6.refs_2_
  30.0 0.0 copy-start.3
  30.0 0.5 %advection_kernel.2 = (f32[128,256]{1,0:T(8,128)S(1)}, f32[128,256]{1,0:T(8,128)S(1)}, f32[128,256]{1,0:T(8,128)S(1)}, f32[128,256]{1,0:T(8,128)S(1)}) custom-call(f32[256,768]{1,0:T(8,128)S(1)} %get-tuple-element.22.refs_0_, f32[128,768]{1,0:T(8,128)S(1)} %pack_kernel.2.refs_1_, f32[128,768]{1,0:T(8,128)S(1)} %collective-permute-done.6.refs_2_, ...), custom_call_target="tpu_custom_call" | custom-call | flops 201326592 | bytes 3145728 | tf_op jit(solution)/shard_map/advection_kernel/pallas_call | solution.py:555
  30.5 1.5 %collective-permute-start.7 = (f32[128,256]{1,0:T(8,128)S(1)}, f32[128,256]{1,0:T(8,128)S(1)}, u32[]{:S(2)}, u32[]{:S(2)}) collective-permute-start(f32[128,256]{1,0:T(8,128)S(1)} %get-tuple-element.26), channel_id=1, source_target_pairs={{0,1},{1,0},{2,3},{3,2},{4,5},{5,4},{6,7},{7,6},{8,9},{9,8},{10,11... | collective-permute-start | bytes 393224 | tf_op jit(solution)/shard_map/ppermute | solution.py:568
  32.0 0.5 %collective-permute-start.8 = (f32[128,256]{1,0:T(8,128)S(1)}, f32[128,256]{1,0:T(8,128)S(1)}, u32[]{:S(2)}, u32[]{:S(2)}) collective-permute-start(f32[128,256]{1,0:T(8,128)S(1)} %get-tuple-element.27), channel_id=1, source_target_pairs={{0,2},{1,3},{2,0},{3,1},{4,6},{5,7},{6,4},{7,5},{8,10},{9,11},{10,... | collective-permute-start | bytes 393224 | tf_op jit(solution)/shard_map/ppermute | solution.py:568
  32.5 0.3 collective-permute-done.14.refs_1_
  32.8 1.4 %collective-permute-start.9 = (f32[128,256]{1,0:T(8,128)S(1)}, f32[128,256]{1,0:T(8,128)S(1)}, u32[]{:S(2)}, u32[]{:S(2)}) collective-permute-start(f32[128,256]{1,0:T(8,128)S(1)} %get-tuple-element.28), channel_id=1, source_target_pairs={{0,3},{1,2},{2,1},{3,0},{4,7},{5,6},{6,5},{7,4},{8,11},{9,10},{10,... | collective-permute-start | bytes 393224 | tf_op jit(solution)/shard_map/ppermute | solution.py:568
  34.2 2.9 %collective-permute-done.15.refs_2_ = f32[128,256]{1,0:T(8,128)S(1)} collective-permute-done((f32[128,256]{1,0:T(8,128)S(1)}, f32[128,256]{1,0:T(8,128)S(1)}, u32[]{:S(2)}, u32[]{:S(2)}) %collective-permute-start.15) | collective-permute-done | bytes 131104 | tf_op jit(solution)/shard_map/ppermute | solution.py:568
  37.1 0.0 collective-permute-done.16.refs_3_
  37.1 0.0 copy-done.3
  37.1 1.4 %first_kernel.1.refs_5_ = f32[2,1,4,64,512]{4,3,2,1,0:T(8,128)S(1)} custom-call(f32[128,256]{1,0:T(8,128)S(1)} %get-tuple-element.30.refs_0_, f32[128,256]{1,0:T(8,128)S(1)} %collective-permute-done.14.refs_1_, f32[128,256]{1,0:T(8,128)S(1)} %collective-permute-done.15.refs_2_, f32[128,256]{1,0:T(8,128)S(1)} %collective-permute-done.16.refs_3_, ...), custom_call_target="tpu_custom_call" | custom-call | flops 402653184 | bytes 4718592 | tf_op jit(solution)/shard_map/first_kernel/pallas_call | solution.py:555
  38.5 0.2 collective-permute-done.7.refs_1_
  38.7 3.3 %collective-permute-done.8.refs_2_ = f32[128,256]{1,0:T(8,128)S(1)} collective-permute-done((f32[128,256]{1,0:T(8,128)S(1)}, f32[128,256]{1,0:T(8,128)S(1)}, u32[]{:S(2)}, u32[]{:S(2)}) %collective-permute-start.8) | collective-permute-done | bytes 131104 | tf_op jit(solution)/shard_map/ppermute | solution.py:568
  42.0 0.0 collective-permute-done.9.refs_3_
  42.0 2.4 %second_kernel.1 = (f32[2,1,4,64,512]{4,3,2,1,0:T(8,128)}, f32[2,1,4,64,512]{4,3,2,1,0:T(8,128)}) custom-call(f32[128,256]{1,0:T(8,128)S(1)} %get-tuple-element.25.refs_0_, f32[128,256]{1,0:T(8,128)S(1)} %collective-permute-done.7.refs_1_, f32[128,256]{1,0:T(8,128)S(1)} %collective-permute-done.8.refs_2_, f32[128,256]{1,0:T(8,128)S(1)} %collective-permute-done.9.refs_3_, ...), custom_call_target="tpu_custom_call" | custom-call | flops 402653184 | bytes 5767168 | tf_op jit(solution)/shard_map/second_kernel/pallas_call | solution.py:555
  (5 shorter events, 0.1 us)
Async XLA Ops:
  0.6 1.0 %copy-start.4 = (f32[6,4,64,32]{2,3,1,0:T(8,128)S(1)}, f32[6,4,64,32]{2,3,1,0:T(8,128)}, u32[]{:S(2)}) copy-start(f32[6,4,64,32]{2,3,1,0:T(8,128)} %param.7) | copy-start | bytes 589828
  1.7 8.0 %collective-permute-start.10 = (f32[32,768]{1,0:T(8,128)S(1)}, f32[32,768]{1,0:T(8,128)S(1)}, u32[]{:S(2)}, u32[]{:S(2)}) collective-permute-start(f32[32,768]{1,0:T(8,128)S(1)} %get-tuple-element.29.refs_0_), channel_id=1, source_target_pairs={{0,24},{4,28},{8,16},{12,20},{16,8},{20,12},{24,0},{28,4},{1,25},{... | collective-permute-start | bytes 294920 | tf_op jit(solution)/shard_map/ppermute | solution.py:568
  6.9 1.2 %copy-start = (f32[2,1,4,64,512]{4,3,2,1,0:T(8,128)S(1)}, f32[2,1,4,64,512]{4,3,2,1,0:T(8,128)}, u32[]{:S(2)}) copy-start(f32[2,1,4,64,512]{4,3,2,1,0:T(8,128)} %refs_4_.4) | copy-start | bytes 3145732
  8.1 3.6 %copy-start.1 = (f32[2,1,4,64,512]{4,3,2,1,0:T(8,128)S(1)}, f32[2,1,4,64,512]{4,3,2,1,0:T(8,128)}, u32[]{:S(2)}) copy-start(f32[2,1,4,64,512]{4,3,2,1,0:T(8,128)} %refs_4_.4) | copy-start | bytes 3145732
  8.1 5.0 %collective-permute-start.1 = (f32[40,768]{1,0:T(8,128)S(1)}, f32[40,768]{1,0:T(8,128)S(1)}, u32[]{:S(2)}, u32[]{:S(2)}) collective-permute-start(f32[40,768]{1,0:T(8,128)S(1)} %lines_kernel.1.refs_1_), channel_id=1, source_target_pairs={{0,1},{1,0},{2,3},{3,2},{4,5},{5,4},{6,7},{7,6},{8,9},{9,8},{10,11... | collective-permute-start | bytes 368648 | tf_op jit(solution)/shard_map/ppermute | solution.py:568
  9.7 7.5 %collective-permute-start.11 = (f32[32,768]{1,0:T(8,128)S(1)}, f32[32,768]{1,0:T(8,128)S(1)}, u32[]{:S(2)}, u32[]{:S(2)}) collective-permute-start(f32[32,768]{1,0:T(8,128)S(1)} %get-tuple-element.29.refs_0_), channel_id=1, source_target_pairs={{0,8},{4,12},{8,0},{12,4},{16,24},{20,28},{24,16},{28,20},{1,9},{5... | collective-permute-start | bytes 294920 | tf_op jit(solution)/shard_map/ppermute | solution.py:568
  9.8 7.4 %collective-permute-start.12 = (f32[32,768]{1,0:T(8,128)S(1)}, f32[32,768]{1,0:T(8,128)S(1)}, u32[]{:S(2)}, u32[]{:S(2)}) collective-permute-start(f32[32,768]{1,0:T(8,128)S(1)} %collective-permute-done.10.refs_1_), channel_id=1, source_target_pairs={{0,8},{4,12},{8,0},{12,4},{16,24},{20,28},{24,16},{28,20},{1,9},{5... | collective-permute-start | bytes 294920 | tf_op jit(solution)/shard_map/ppermute | solution.py:568
  11.7 10.2 %collective-permute-start = (f32[136,512]{1,0:T(8,128)S(1)}, f32[136,512]{1,0:T(8,128)S(1)}, u32[]{:S(2)}, u32[]{:S(2)}) collective-permute-start(f32[136,512]{1,0:T(8,128)S(1)} %near_x_kernel.1), channel_id=1, source_target_pairs={{0,1},{1,0},{2,3},{3,2},{4,5},{5,4},{6,7},{7,6},{8,9},{9,8},{10,11... | collective-permute-start | bytes 835592 | tf_op jit(solution)/shard_map/ppermute | solution.py:568
  13.1 8.9 %collective-permute-start.2 = (f32[136,512]{1,0:T(8,128)S(1)}, f32[136,512]{1,0:T(8,128)S(1)}, u32[]{:S(2)}, u32[]{:S(2)}) collective-permute-start(f32[136,512]{1,0:T(8,128)S(1)} %get-tuple-element.19), channel_id=1, source_target_pairs={{0,2},{1,3},{2,0},{3,1},{4,6},{5,7},{6,4},{7,5},{8,10},{9,11},{10,... | collective-permute-start | bytes 835592 | tf_op jit(solution)/shard_map/ppermute | solution.py:568
  14.7 2.6 %copy-start.2 = (bf16[4,256,512]{2,1,0:T(8,128)(2,1)S(1)}, bf16[4,256,512]{2,1,0:T(8,128)(2,1)}, u32[]{:S(2)}) copy-start(bf16[4,256,512]{2,1,0:T(8,128)(2,1)} %constant.4.clone.refs_1_.refs_4_.refs_3_.refs_6_) | copy-start | bytes 3145732
  14.7 6.5 %collective-permute-start.3 = (f32[32,768]{1,0:T(8,128)S(1)}, f32[32,768]{1,0:T(8,128)S(1)}, u32[]{:S(2)}, u32[]{:S(2)}) collective-permute-start(f32[32,768]{1,0:T(8,128)S(1)} %get-tuple-element.23.refs_0_), channel_id=1, source_target_pairs={{0,24},{4,28},{8,16},{12,20},{16,8},{20,12},{24,0},{28,4},{1,25},{... | collective-permute-start | bytes 294920 | tf_op jit(solution)/shard_map/ppermute | solution.py:568
  17.2 4.7 %copy-start.5 = (bf16[4,2,256,256]{3,2,1,0:T(8,128)(2,1)S(1)}, bf16[4,2,256,256]{3,2,1,0:T(8,128)(2,1)}, u32[]{:S(2)}) copy-start(bf16[4,2,256,256]{3,2,1,0:T(8,128)(2,1)} %constant.5.clone.refs_5_) | copy-start | bytes 3145732
  17.2 8.7 %collective-permute-start.13 = (f32[128,768]{1,0:T(8,128)S(1)}, f32[128,768]{1,0:T(8,128)S(1)}, u32[]{:S(2)}, u32[]{:S(2)}) collective-permute-start(f32[128,768]{1,0:T(8,128)S(1)} %pack_kernel.3.refs_1_), channel_id=1, source_target_pairs={{0,4},{4,0},{8,12},{12,8},{16,20},{20,16},{24,28},{28,24},{1,5},{5... | collective-permute-start | bytes 1179656 | tf_op jit(solution)/shard_map/ppermute | solution.py:568
  18.2 6.1 %collective-permute-start.4 = (f32[32,768]{1,0:T(8,128)S(1)}, f32[32,768]{1,0:T(8,128)S(1)}, u32[]{:S(2)}, u32[]{:S(2)}) collective-permute-start(f32[32,768]{1,0:T(8,128)S(1)} %get-tuple-element.23.refs_0_), channel_id=1, source_target_pairs={{0,8},{4,12},{8,0},{12,4},{16,24},{20,28},{24,16},{28,20},{1,9},{5... | collective-permute-start | bytes 294920 | tf_op jit(solution)/shard_map/ppermute | solution.py:568
  21.2 4.6 %collective-permute-start.5 = (f32[32,768]{1,0:T(8,128)S(1)}, f32[32,768]{1,0:T(8,128)S(1)}, u32[]{:S(2)}, u32[]{:S(2)}) collective-permute-start(f32[32,768]{1,0:T(8,128)S(1)} %collective-permute-done.3.refs_1_), channel_id=1, source_target_pairs={{0,8},{4,12},{8,0},{12,4},{16,24},{20,28},{24,16},{28,20},{1,9},{5... | collective-permute-start | bytes 294920 | tf_op jit(solution)/shard_map/ppermute | solution.py:568
  25.9 4.1 %collective-permute-start.6 = (f32[128,768]{1,0:T(8,128)S(1)}, f32[128,768]{1,0:T(8,128)S(1)}, u32[]{:S(2)}, u32[]{:S(2)}) collective-permute-start(f32[128,768]{1,0:T(8,128)S(1)} %pack_kernel.2.refs_1_), channel_id=1, source_target_pairs={{0,4},{4,0},{8,12},{12,8},{16,20},{20,16},{24,28},{28,24},{1,5},{5... | collective-permute-start | bytes 1179656 | tf_op jit(solution)/shard_map/ppermute | solution.py:568
  26.4 6.4 %collective-permute-start.14 = (f32[128,256]{1,0:T(8,128)S(1)}, f32[128,256]{1,0:T(8,128)S(1)}, u32[]{:S(2)}, u32[]{:S(2)}) collective-permute-start(f32[128,256]{1,0:T(8,128)S(1)} %get-tuple-element.31), channel_id=1, source_target_pairs={{0,1},{1,0},{2,3},{3,2},{4,5},{5,4},{6,7},{7,6},{8,9},{9,8},{10,11... | collective-permute-start | bytes 393224 | tf_op jit(solution)/shard_map/ppermute | solution.py:568
  28.0 9.1 %collective-permute-start.15 = (f32[128,256]{1,0:T(8,128)S(1)}, f32[128,256]{1,0:T(8,128)S(1)}, u32[]{:S(2)}, u32[]{:S(2)}) collective-permute-start(f32[128,256]{1,0:T(8,128)S(1)} %get-tuple-element.32), channel_id=1, source_target_pairs={{0,2},{1,3},{2,0},{3,1},{4,6},{5,7},{6,4},{7,5},{8,10},{9,11},{10,... | collective-permute-start | bytes 393224 | tf_op jit(solution)/shard_map/ppermute | solution.py:568
  28.5 8.6 %collective-permute-start.16 = (f32[128,256]{1,0:T(8,128)S(1)}, f32[128,256]{1,0:T(8,128)S(1)}, u32[]{:S(2)}, u32[]{:S(2)}) collective-permute-start(f32[128,256]{1,0:T(8,128)S(1)} %get-tuple-element.33), channel_id=1, source_target_pairs={{0,3},{1,2},{2,1},{3,0},{4,7},{5,6},{6,5},{7,4},{8,11},{9,10},{10,... | collective-permute-start | bytes 393224 | tf_op jit(solution)/shard_map/ppermute | solution.py:568
  30.0 7.1 %copy-start.3 = (f32[2,1,4,64,512]{4,3,2,1,0:T(8,128)S(1)}, f32[2,1,4,64,512]{4,3,2,1,0:T(8,128)}, u32[]{:S(2)}) copy-start(f32[2,1,4,64,512]{4,3,2,1,0:T(8,128)} %refs_5_.2) | copy-start | bytes 3145732
  30.5 8.2 %collective-permute-start.7 = (f32[128,256]{1,0:T(8,128)S(1)}, f32[128,256]{1,0:T(8,128)S(1)}, u32[]{:S(2)}, u32[]{:S(2)}) collective-permute-start(f32[128,256]{1,0:T(8,128)S(1)} %get-tuple-element.26), channel_id=1, source_target_pairs={{0,1},{1,0},{2,3},{3,2},{4,5},{5,4},{6,7},{7,6},{8,9},{9,8},{10,11... | collective-permute-start | bytes 393224 | tf_op jit(solution)/shard_map/ppermute | solution.py:568
  32.0 10.0 %collective-permute-start.8 = (f32[128,256]{1,0:T(8,128)S(1)}, f32[128,256]{1,0:T(8,128)S(1)}, u32[]{:S(2)}, u32[]{:S(2)}) collective-permute-start(f32[128,256]{1,0:T(8,128)S(1)} %get-tuple-element.27), channel_id=1, source_target_pairs={{0,2},{1,3},{2,0},{3,1},{4,6},{5,7},{6,4},{7,5},{8,10},{9,11},{10,... | collective-permute-start | bytes 393224 | tf_op jit(solution)/shard_map/ppermute | solution.py:568
  32.8 9.2 %collective-permute-start.9 = (f32[128,256]{1,0:T(8,128)S(1)}, f32[128,256]{1,0:T(8,128)S(1)}, u32[]{:S(2)}, u32[]{:S(2)}) collective-permute-start(f32[128,256]{1,0:T(8,128)S(1)} %get-tuple-element.28), channel_id=1, source_target_pairs={{0,3},{1,2},{2,1},{3,0},{4,7},{5,6},{6,5},{7,4},{8,11},{9,10},{10,... | collective-permute-start | bytes 393224 | tf_op jit(solution)/shard_map/ppermute | solution.py:568
